TPU v7x, 32 devices: a whole 2x2x4 slice. The times are simulated.
32 devices in a mesh: section: 2 (over core), group: 4 (over y, x), replica: 4 (over z).
Axes of the slice: x: 2, y: 2, z: 4, core: 2. Of those that a mesh axis runs over, the one named last changes fastest.
Arguments:
- block_input: bfloat16 [8192, 640], P(('group', 'replica')), may hold values from -6 to 6
- cotangent: bfloat16 [8192, 640], P(('group', 'replica')), may hold values from -6 to 6
- crop_count: int32 [16], P(('group', 'replica')), may hold values from 1 to 2, as said below
- mask_count: int32 [32], P(('group', 'replica')), may hold values from 12 to 75
- qkv_weight: bfloat16 [2, 640, 1920], P('section'), may hold values from -0.25 to 0.25
- qkv_bias: float32 [2, 1920], P('section'), may hold values from -1.5 to 1.5
- out_weight: bfloat16 [2, 640, 640], P('section'), may hold values from -2 to 2
- out_bias: float32 [2, 640], P('section'), may hold values from -1.5 to 1.5
- up_weight: bfloat16 [2, 640, 2560], P('section'), may hold values from -0.25 to 0.25
- up_bias: float32 [2, 2560], P('section'), may hold values from -1.5 to 1.5
- down_weight: bfloat16 [2, 2560, 640], P('section'), may hold values from -0.125 to 0.125
- down_bias: float32 [2, 640], P('section'), may hold values from -1.5 to 1.5
- norm_gain: float32 [2, 2, 640], P('section'), may hold values from 0.4 to 1.6
- norm_shift: float32 [2, 2, 640], P('section'), may hold values from -1.5 to 1.5
Outputs:
- activations: bfloat16 [2, 8192, 640], P('section', ('group', 'replica'))
- input_grads: bfloat16 [2, 8192, 640], P('section', ('group', 'replica'))
- grad_qkv_weight: float32 [2, 640, 1920], P('section', 'group')
- grad_qkv_bias: float32 [2, 1920], P('section', 'group')
- grad_out_weight: float32 [2, 640, 640], P('section', 'group')
- grad_out_bias: float32 [2, 640], P('section', 'group')
- grad_up_weight: float32 [2, 640, 2560], P('section', 'group')
- grad_up_bias: float32 [2, 2560], P('section', 'group')
- grad_down_weight: float32 [2, 2560, 640], P('section', 'group')
- grad_down_bias: float32 [2, 640], P('section', 'group')
- grad_norm_gain: float32 [2, 2, 640], P('section', None, 'group')
- grad_norm_shift: float32 [2, 2, 640], P('section', None, 'group')
Inputs may be any that keep to these rules, and one draw needn't show every extreme that they name: The live crops of a data rank fill its first crop_count slots; some rank fills all 2.
All inputs are finite; a program needn't handle non-finite values.
Results may differ from a plain program's by a relative error of at most 0.017.
Values may be sent and summed in bfloat16 or wider, within the bound.
No kernel may reach another device: no remote copies, remote signals or barrier semaphores. Data moves between devices by JAX's collectives and lax.ppermute only.
A program may use at most 256 MiB of HBM per device.

v0:
```python
import jax
import jax.numpy as jnp
import numpy as np
from jax import lax
from jax.experimental import pallas as pl
from jax.experimental.pallas import tpu as pltpu
from jax.sharding import PartitionSpec as P

HEADS = 20
HEAD_DIM = 32
LEN = 256
MASK_MEAN = 38
CROP_DEV = 2
EPSILON = 1e-05
ROTARY_BASE = 10000.0

BF = jnp.bfloat16
F32 = jnp.float32
NN = (((1,), (0,)), ((), ()))
NT = (((1,), (1,)), ((), ()))
TN = (((0,), (0,)), ((), ()))

FIRST_LIMIT, FORWARD_LIMIT, MLP_LIMIT, ATTENTION_LIMIT, QKV_LIMIT = 40, 14, 16, 17, 8
ATTENTION_MICROS = 12
REPLICAS = 4
GROUPS = 4
PAD = 16
ROW_QKV, ROW_OUT, ROW_UP, ROW_DOWN, ROW_GAIN, ROW_SHIFT = 0, 3, 4, 8, 9, 11

ANY = pl.BlockSpec(memory_space=pl.ANY)
HBM = pl.BlockSpec(memory_space=pltpu.HBM)
VMEM = pl.BlockSpec(memory_space=pltpu.VMEM)
SMEM = pl.BlockSpec(memory_space=pltpu.SMEM)


def shape(dims, dtype):
    return jax.ShapeDtypeStruct(dims, dtype)


def mm(left, right, dims=NN):
    return lax.dot_general(left, right, dims, preferred_element_type=F32)


def unit_rows_of(values):
    centred = values - jnp.mean(values, axis=-1, keepdims=True)
    inverse = lax.rsqrt(jnp.mean(centred * centred, axis=-1, keepdims=True) + EPSILON)
    return centred * inverse, inverse


def norm_back(grad, unit, inverse, gain):
    scaled = grad * gain
    return inverse * (
        scaled
        - jnp.mean(scaled, axis=-1, keepdims=True)
        - unit * jnp.mean(scaled * unit, axis=-1, keepdims=True)
    )


def rotary_tables():
    lane = np.arange(128) % HEAD_DIM
    half = HEAD_DIM // 2
    freq = ROTARY_BASE ** (-(lane % half).astype(np.float64) * (2.0 / HEAD_DIM))
    angles = np.arange(LEN)[:, None] * freq[None, :]
    sign = np.where(lane < half, -1.0, 1.0)[None, :]
    return np.stack([np.cos(angles), np.sin(angles) * sign]).astype(np.float32)


def rotary_columns():
    half = HEAD_DIM // 2
    freq = ROTARY_BASE ** (-np.arange(half, dtype=np.float64) * (2.0 / HEAD_DIM))
    angles = freq[:, None] * np.arange(LEN)[None, :]
    return np.stack([np.cos(angles), np.sin(angles)]).astype(np.float32)


def swap_halves(values):
    lane = lax.broadcasted_iota(jnp.int32, values.shape, 1) % HEAD_DIM
    half = HEAD_DIM // 2
    return jnp.where(
        lane < half,
        pltpu.roll(values, 128 - half, axis=1),
        pltpu.roll(values, half, axis=1),
    )


def head_stack(block, per):
    head = lax.broadcasted_iota(jnp.int32, block.shape, 1) // HEAD_DIM
    return jnp.concatenate(
        [jnp.where(head == h, block, jnp.zeros_like(block)) for h in range(per)], axis=0
    )


class Copies:
    def __init__(self, sems):
        self.sems = sems
        self.used = 0
        self.open = []

    def start(self, src, dst):
        copy = pltpu.make_async_copy(src, dst, self.sems.at[self.used])
        self.used += 1
        copy.start()
        return copy

    def save(self, src, dst):
        self.open.append(self.start(src, dst))

    def finish(self):
        for copy in self.open:
            copy.wait()


def call(kernel, outs, ins, scratch, sems, aliases, name, after=None, limit=16, spaces=None, out_spaces=None, micros=0.1):
    count = len(ins)
    places = {"v": VMEM, "h": HBM, "a": ANY, "s": SMEM}
    spaces = spaces or "v" * count
    out_spaces = out_spaces or "v" * len(outs)
    in_specs = [SMEM if a.ndim == 1 else places[p] for a, p in zip(ins, spaces)]
    ins = [pltpu.with_memory_space_constraint(a, pltpu.HBM) if p == "h" else a for a, p in zip(ins, spaces)]
    body = kernel
    if after is not None:
        ins = list(ins) + [after]
        in_specs = in_specs + [ANY]

        def body(*refs):
            kernel(*refs[:count], *refs[count + 1 :])

    outs = [pltpu.HBM(o.shape, o.dtype) if p == "h" else o for o, p in zip(outs, out_spaces)]
    return pl.pallas_call(
        body,
        out_shape=outs,
        in_specs=in_specs,
        out_specs=[places[p] for p in out_spaces],
        scratch_shapes=scratch + ([pltpu.SemaphoreType.DMA((sems,))] if sems else []),
        input_output_aliases=aliases,
        compiler_params=pltpu.CompilerParams(vmem_limit_bytes=limit << 20),
        cost_estimate=pl.CostEstimate(
            flops=int(micros * 1.15e9), bytes_accessed=0, transcendentals=0
        ),
        name=name,
    )(*ins)


TOKEN = jax.ShapeDtypeStruct((8, 128), F32)


def vmem_like(arr):
    return pltpu.VMEM(arr.shape, arr.dtype)


def forward(slot, info, live, own, arrived, params, tab, act, after=None):
    qkvw, qkvb, outw, outb, upw, upb, downw, downb, gain, shift = params
    dim = own.shape[1]
    blocks = dim // 128
    wide = upw.shape[1]
    parts = wide // dim
    per = 128 // HEAD_DIM
    manual = slot == 0
    saved = [
        shape((LEN, dim), BF),
        shape((LEN, 3 * dim), BF),
        shape((HEADS, LEN, LEN), BF),
        shape((dim, LEN), BF),
        shape((LEN, dim), F32),
        shape((LEN, wide), BF),
        shape((LEN, wide), BF),
    ]
    weights = [qkvb, outb, upb, downb, gain, shift, tab, qkvw, outw, upw, downw]
    sources = [own] if slot == 0 else [arrived] if slot == 2 else [own, arrived]
    before = [] if act is None else [act]
    ins = [info, live] + sources + weights + before
    count = len(sources)

    def kernel(info, live, *refs):
        xs = refs[:count]
        given = refs[count : count + 11]
        act_h, *outs = refs[count + 11 + len(before) : count + 19 + len(before)]
        scratch = refs[count + 19 + len(before) :]
        act_s, vt_s, score_s, up_s = scratch[:4]
        sems = scratch[-1]
        y_s, qkv_s, prob_s, mixt_s, mid_s, gp_s, hid_s = outs
        used = scratch[4:-1] if manual else xs[-1:] + given
        qkvb, outb, upb, downb, gain, shift, tab, qkvw, outw, upw, downw = used[1:]
        crop = slot - info[0]

        @pl.when(jnp.logical_and(crop >= 0, crop < CROP_DEV))
        def _():
            copies = Copies(sems)
            heavy = []
            if manual:
                rows = xs[0].at[pl.ds(0, LEN)]
                loads = [copies.start(h, s) for h, s in zip((rows,) + given, used)]
                heavy = loads[8:]
                wait_all(loads[:8])
                x = used[0][...].astype(F32)
            elif slot == 1:
                x = jnp.where(info[0] == 0, xs[0][LEN:, :], xs[1][...]).astype(F32)
            else:
                x = xs[0][...].astype(F32)

            def ready(index):
                if manual:
                    heavy[index].wait()

            unit, _ = unit_rows_of(x)
            normed = (unit * gain[0:1, :] + shift[0:1, :]).astype(BF)
            ready(0)
            third = mm(normed, qkvw[:, 2 * dim :]) + qkvb[:, 2 * dim :]
            low = third.astype(BF)
            qkv_s[:, 2 * dim :] = low
            vt_s[...] = low.T
            for part in range(2):
                third = mm(normed, qkvw[:, part * dim : (part + 1) * dim])
                third = third + qkvb[:, part * dim : (part + 1) * dim]
                for j in range(blocks):
                    b = third[:, 128 * j : 128 * j + 128]
                    b = b * tab[0] + swap_halves(b) * tab[1]
                    if part == 0:
                        b = b * HEAD_DIM**-0.5
                    at = part * dim + 128 * j
                    qkv_s[:, at : at + 128] = b.astype(BF)
            for j in range(blocks):
                q = qkv_s[:, 128 * j : 128 * j + 128]
                k = qkv_s[:, dim + 128 * j : dim + 128 * j + 128]
                score_s[per * LEN * j : per * LEN * (j + 1), :] = mm(head_stack(k, per), q, NT)

            def soft(h, _):
                s = score_s[pl.ds(pl.multiple_of(h * LEN, LEN), LEN), :]
                e = jnp.exp(s - jnp.max(s, axis=0, keepdims=True))
                prob_s[h] = (e * (1.0 / jnp.sum(e, axis=0, keepdims=True))).astype(BF)
                return 0

            lax.fori_loop(0, HEADS, soft, 0, unroll=2)
            for h in range(HEADS):
                at = slice(HEAD_DIM * h, HEAD_DIM * (h + 1))
                mixt_s[at, :] = mm(vt_s[at, :], prob_s[h]).astype(BF)
            ready(1)
            mid = x + mm(mixt_s[...], outw[...], TN) + outb[...]
            mid_s[...] = mid
            unit, _ = unit_rows_of(mid)
            normed = (unit * gain[1:2, :] + shift[1:2, :]).astype(BF)
            ready(2)
            up_s[...] = mm(normed, upw[...])
            for c in range(parts):
                cols = slice(c * dim, (c + 1) * dim)
                u = up_s[:, cols] + upb[:, cols]
                cdf = 0.5 + 0.5 * lax.erf(u * 0.5**0.5)
                hid_s[:, cols] = (u * cdf).astype(BF)
                gp_s[:, cols] = (
                    cdf + u * (jnp.exp(u * u * -0.5) * (2 * np.pi) ** -0.5)
                ).astype(BF)
            ready(3)
            low = (mid_s[...] + downb[...] + mm(hid_s[...], downw[...])).astype(BF)
            y_s[...] = low
            act_s[...] = jnp.where(crop < live[0], low, jnp.zeros_like(low))
            at = pl.multiple_of(crop * LEN, LEN)
            copies.save(act_s, act_h.at[pl.ds(at, LEN)])
            copies.finish()

    outs = [shape(own.shape, BF)] + saved
    scratch = [
        pltpu.VMEM((LEN, dim), BF),
        pltpu.VMEM((dim, LEN), BF),
        pltpu.VMEM((HEADS * LEN, LEN), F32),
        pltpu.VMEM((LEN, wide), F32),
    ]
    if manual:
        scratch += [pltpu.VMEM((LEN, dim), BF)] + [vmem_like(a) for a in weights]
    aliases = {} if act is None else {len(ins) - 1: 0}
    spaces = "ss" + ("h" if manual else "v") * (count + 11) + "h" * len(before)
    out = call(
        kernel,
        outs,
        ins,
        scratch,
        16,
        aliases,
        "layer_forward",
        after,
        FIRST_LIMIT if manual else FORWARD_LIMIT,
        spaces,
        "h" + "v" * 7,
    )
    return out[0], out[1:]


def crop_weight(live, masks, crop, section):
    if section == 0:
        return 1.0
    count = jnp.where(live[0] > crop, masks[crop], 0)
    return jnp.full((1, 1), count, jnp.int32).astype(F32) / MASK_MEAN


def add_row(ref, row, values):
    ref[row : row + 1, :] = ref[row : row + 1, :] + jnp.sum(values, axis=0, keepdims=True)


def lay_out(own, bit, keep, send, block, index, row, count, at):
    src = pl.ds(row if isinstance(row, int) else pl.multiple_of(row, PAD), count)
    dst = pl.ds(at if isinstance(at, int) else pl.multiple_of(at, PAD), count)
    mine = own == bit

    @pl.when(mine)
    def _():
        keep[dst, :] = block[index, src, :]

    @pl.when(jnp.logical_not(mine))
    def _():
        send[dst, :] = block[index, src, :]


def keep_given(active, given, bufs):
    @pl.when(jnp.logical_not(active))
    def _():
        for old, new in zip(given, bufs):
            new[...] = old[...]


def pair_shapes(rows, dim):
    return [shape((rows, dim), BF)] * 2


def joined(refs, cols):
    return jnp.concatenate([r[:, cols] for r in refs], axis=0)


def wait_all(copies):
    for copy in copies:
        copy.wait()


def mlp_grad(section, info, live, masks, g, saved, params, after):
    mixts = [s[3] for s in saved]
    mids, gps, hids = ([s[k] for s in saved] for k in (4, 5, 6))
    upw, downw, gain, shift = params[4], params[6], params[8], params[9]
    rows, dim = g.shape
    wide = upw.shape[1]
    parts = wide // dim
    crops = len(saved)
    share = dim // GROUPS
    ins = [info, live, masks, g, gain, shift, downw, upw] + mids + gps + hids + mixts

    def kernel(info, live, masks, g_s, gain, shift, downw, upw, *refs):
        mid_s, gp_s, hid_s, mixt_s = (refs[i * crops : (i + 1) * crops] for i in range(4))
        refs = refs[4 * crops :]
        send_a, keep_a, send_b, keep_b, gmid_s, small_s = refs[:6]
        gu_s, block_s, low_s, normt_s, back_s = refs[7:]

        @pl.when(info[0] == section)
        def _():
            small_s[...] = jnp.zeros_like(small_s)
            for c in range(crops):
                crop = slice(c * LEN, (c + 1) * LEN)
                grad = g_s[crop, :].astype(F32) * crop_weight(live, masks, c, section)
                low = grad.astype(BF)
                low_s[crop, :] = low
                add_row(small_s, ROW_DOWN, low.astype(F32))
                unit, _ = unit_rows_of(mid_s[c][...])
                normt_s[:, crop] = (unit * gain[1:2, :] + shift[1:2, :]).astype(BF).T
            for c in range(parts):
                cols = slice(c * dim, (c + 1) * dim)
                block_s[c] = mm(joined(hid_s, cols), low_s[...], TN).astype(BF)

            @pl.loop(0, GROUPS * parts)
            def _(i):
                shard, row = i // parts, (i % parts) * share
                at = (shard // 2) * dim + row
                lay_out(info[1], shard % 2, keep_a, send_a, block_s, shard, row, share, at)

            for c in range(parts):
                cols = slice(c * dim, (c + 1) * dim)
                grad_up = mm(low_s[...], downw[cols, :], NT) * joined(gp_s, cols).astype(F32)
                grad_up = grad_up.astype(BF)
                gu_s[:, cols] = grad_up
                small_s[ROW_UP + c : ROW_UP + c + 1, :] = jnp.sum(
                    grad_up.astype(F32), axis=0, keepdims=True
                )
            back_s[...] = mm(gu_s[...], upw[...], NT)
            for c in range(crops):
                crop = slice(c * LEN, (c + 1) * LEN)
                grad = g_s[crop, :].astype(F32) * crop_weight(live, masks, c, section)
                unit, inverse = unit_rows_of(mid_s[c][...])
                back = back_s[crop, :]
                gmid = grad + norm_back(back, unit, inverse, gain[1:2, :])
                gmid_s[crop, :] = gmid
                low = gmid.astype(BF)
                low_s[crop, :] = low
                add_row(small_s, ROW_GAIN + 1, back * unit)
                add_row(small_s, ROW_SHIFT + 1, back)
                add_row(small_s, ROW_OUT, low.astype(F32))
            for c in range(parts):
                block_s[c] = mm(normt_s[...], gu_s[:, c * dim : (c + 1) * dim]).astype(BF)
            mixt = jnp.concatenate([m[...] for m in mixt_s], axis=1)
            block_s[parts] = mm(mixt, low_s[...]).astype(BF)

            @pl.loop(0, GROUPS * (parts + 1))
            def _(i):
                shard, c = i // (parts + 1), i % (parts + 1)
                at = ((shard % 2) * (parts + 1) + c) * share
                lay_out(info[2], shard // 2, keep_b, send_b, block_s, c, shard * share, share, at)

    scratch = [
        pltpu.VMEM((rows, wide), BF),
        pltpu.VMEM((parts + 1, dim, dim), BF),
        pltpu.VMEM((rows, dim), BF),
        pltpu.VMEM((dim, rows), BF),
        pltpu.VMEM((rows, dim), F32),
    ]
    outs = pair_shapes(2 * dim, dim) + pair_shapes(2 * (parts + 1) * share, dim)
    outs += [shape((rows, dim), F32), shape((PAD, dim), F32), TOKEN]
    out = call(kernel, outs, ins, scratch, 0, {}, "mlp_grad", after, MLP_LIMIT, micros=10)
    return out[:4], out[4], out[5], out[6]


def rotate_back(block, tab_t):
    half = HEAD_DIM // 2
    cos, sin = tab_t[0], tab_t[1]
    out = []
    for at in range(0, block.shape[0], HEAD_DIM):
        a, b = block[at : at + half], block[at + half : at + HEAD_DIM]
        out += [a * cos + b * sin, b * cos - a * sin]
    return jnp.concatenate(out, axis=0)


def attention_grad(section, info, gmid, small, xs, saved, params, tab_t, before, after):
    qkvs, probs, mixts = [s[1] for s in saved], [s[2] for s in saved], [s[3] for s in saved]
    qkvw, outw, gain, shift = params[0], params[2], params[8], params[9]
    rows, dim = gmid.shape
    blocks = dim // 128
    per = 128 // HEAD_DIM
    crops = len(saved)
    given = [] if before is None else [before]
    ins = [info, gmid, outw, small, gain, shift, tab_t, qkvw]
    ins += qkvs + probs + mixts + list(xs) + given

    def kernel(info, gmid_s, outw, small_s, gain, shift, tab_t, qkvw, *refs):
        qkv_s, prob_s, mixt_s = (refs[i * crops : (i + 1) * crops] for i in range(3))
        x_s = refs[3 * crops : 3 * crops + len(xs)]
        old = refs[3 * crops + len(xs) : 3 * crops + len(xs) + len(given)]
        refs = refs[3 * crops + len(xs) + len(given) :]
        keep_given(info[0] == section, old, refs[:1])
        dx_s, gqkv_s, normt_s, small_out = refs[:4]
        gmt_s, delta_s, da_s, ds_s, dt_s, kt_s = refs[5:]

        @pl.when(info[0] == section)
        def _():
            low = gmid_s[...].astype(BF)
            gmt_s[...] = mm(outw[...], low, NT).astype(BF)
            for c in range(crops):
                crop = slice(c * LEN, (c + 1) * LEN)
                qkv, prob = qkv_s[c], prob_s[c]
                product = gmt_s[:, crop].astype(F32) * mixt_s[c][...].astype(F32)
                delta_s[...] = jnp.sum(product.reshape(HEADS, HEAD_DIM, LEN), axis=1)[:, None, :]
                kt_s[0] = qkv[:, dim : 2 * dim].T
                kt_s[1] = qkv[:, :dim].T
                for j in range(blocks):
                    v = qkv[:, 2 * dim + 128 * j : 2 * dim + 128 * j + 128]
                    da_s[per * LEN * j : per * LEN * (j + 1), :] = mm(
                        head_stack(v, per), gmt_s[128 * j : 128 * j + 128, crop]
                    )

                def scores(h, _):
                    da = da_s[pl.ds(pl.multiple_of(h * LEN, LEN), LEN), :]
                    ds_s[h] = (prob[h].astype(F32) * (da - delta_s[h])).astype(BF)
                    return 0

                lax.fori_loop(0, HEADS, scores, 0, unroll=2)
                for h in range(HEADS):
                    at = slice(HEAD_DIM * h, HEAD_DIM * (h + 1))
                    dt_s[0, at, :] = mm(kt_s[0, at, :], ds_s[h])
                    dt_s[1, at, :] = mm(kt_s[1, at, :], ds_s[h], NT)
                    dt_s[2, at, :] = mm(gmt_s[at, crop], prob[h], NT)
                dq = rotate_back(dt_s[0] * HEAD_DIM**-0.5, tab_t)
                gqkv_s[crop, :dim] = dq.astype(BF).T
                gqkv_s[crop, dim : 2 * dim] = rotate_back(dt_s[1], tab_t).astype(BF).T
                gqkv_s[crop, 2 * dim :] = dt_s[2].astype(BF).T
            unit, inverse = unit_rows_of(joined(x_s, slice(None)).astype(F32))
            normt_s[...] = (unit * gain[0:1, :] + shift[0:1, :]).astype(BF).T
            back = mm(gqkv_s[...], qkvw[...], NT)
            dx_s[...] = (gmid_s[...] + norm_back(back, unit, inverse, gain[0:1, :])).astype(BF)
            small_out[...] = small_s[...]
            small_out[ROW_GAIN : ROW_GAIN + 1, :] = jnp.sum(back * unit, axis=0, keepdims=True)
            small_out[ROW_SHIFT : ROW_SHIFT + 1, :] = jnp.sum(back, axis=0, keepdims=True)

    outs = [
        shape((rows, dim), BF),
        shape((rows, 3 * dim), BF),
        shape((dim, rows), BF),
        shape(small.shape, F32),
        TOKEN,
    ]
    scratch = [
        pltpu.VMEM((dim, rows), BF),
        pltpu.VMEM((HEADS, 1, LEN), F32),
        pltpu.VMEM((HEADS * LEN, LEN), F32),
        pltpu.VMEM((HEADS, LEN, LEN), BF),
        pltpu.VMEM((3, dim, LEN), F32),
        pltpu.VMEM((2, dim, LEN), BF),
    ]
    aliases = {len(ins) - 1: 0} if given else {}
    out = call(kernel, outs, ins, scratch, 0, aliases, "attention_grad", after, ATTENTION_LIMIT, micros=ATTENTION_MICROS)
    return out[0], out[1:4], out[4]


def qkv_grad(section, info, kept, before, after):
    gqkv, normt, small = kept
    dim, rows = normt.shape
    share = dim // GROUPS
    half = 3 * share // 2
    given = [] if before is None else list(before)
    ins = [info, gqkv, normt, small] + given

    def kernel(info, gqkv_s, normt_s, small_s, *refs):
        old = refs[: len(given)]
        bufs = refs[len(given) : len(given) + 4]
        send_a, keep_a, send_b, keep_b = bufs
        (block_s,) = refs[len(given) + 5 :]
        keep_given(info[0] == section, old, bufs)

        @pl.when(info[0] == section)
        def _():
            sums = [
                jnp.sum(gqkv_s[:, c * dim : (c + 1) * dim].astype(F32), axis=0, keepdims=True)
                for c in range(3)
            ]
            tail = jnp.concatenate(sums + [small_s[ROW_OUT:, :]], axis=0).astype(BF)
            send_a[2 * half :, :] = tail
            keep_a[2 * half :, :] = tail
            for c in range(3):
                block_s[c] = mm(normt_s[...], gqkv_s[:, c * dim : (c + 1) * dim]).astype(BF)

            @pl.loop(0, GROUPS)
            def _(shard):
                x, y, base = shard % 2, shard // 2, shard * share
                for c in range(3):
                    row, at, left = 0, c * share, share
                    while left:
                        count = min(left, half - at % half)
                        if at < half:
                            own, bit, keep, send, to = info[1], x, keep_a, send_a, y * half + at
                        else:
                            own, bit, keep, send, to = info[2], y, keep_b, send_b, x * half + at - half
                        lay_out(own, bit, keep, send, block_s, c, base + row, count, to)
                        row, at, left = row + count, at + count, left - count

    scratch = [pltpu.VMEM((3, dim, dim), BF)]
    aliases = {len(ins) - 4 + i: i for i in range(4)} if given else {}
    outs = pair_shapes(2 * half + PAD, dim) + pair_shapes(2 * half, dim) + [TOKEN]
    out = call(kernel, outs, ins, scratch, 0, aliases, "qkv_grad", after, QKV_LIMIT)
    return out[:4], out[4]


STEP = 80


def plus(one, two):
    return (one.astype(F32) + two.astype(F32)).astype(BF)


def add_rows(out, at, one, two, start, count):
    whole = count // STEP * STEP

    @pl.loop(0, whole // STEP)
    def _(i):
        src = pl.ds(pl.multiple_of(start + i * STEP, PAD), STEP)
        dst = pl.ds(pl.multiple_of(at + i * STEP, PAD), STEP)
        out[dst, :] = plus(one[src, :], two[src, :])

    if count > whole:
        src = pl.ds(pl.multiple_of(start + whole, PAD), count - whole)
        out[pl.ds(at + whole, count - whole), :] = plus(one[src, :], two[src, :])


def vmem_call(kernel, outs, ins, name, after, scratch=()):
    return call(kernel, outs, ins, list(scratch), 0, {}, name, after, 8)


def first_sum(info, sets, after):
    dim = sets[0][0].shape[1]
    sizes = [(k.shape[0] // (2 * PAD) * PAD, k.shape[0] % (2 * PAD)) for k in sets[0][::2]]

    def kernel(info, *refs):
        sa, na, sb, nb = refs[4 * len(sets) :]
        for section in range(len(sets)):
            ka, ra, kb, rb = refs[4 * section : 4 * section + 4]
            active = info[0] == section if len(sets) > 1 else info[0] >= 0

            @pl.when(active)
            def _():
                for own, one, two, new, out, (half, extra) in (
                    (info[2], ka, ra, na, sa, sizes[0]),
                    (info[1], kb, rb, nb, sb, sizes[1]),
                ):
                    add_rows(out, 0, one, two, (1 - own) * half, half)
                    add_rows(new, 0, one, two, own * half, half)
                    if extra:
                        tail = plus(one[2 * half :, :], two[2 * half :, :])
                        new[half:, :] = tail
                        out[half:, :] = tail

    outs = [shape((sum(size), dim), BF) for size in sizes for _ in range(2)]
    return vmem_call(kernel, outs, [info] + [a for s in sets for a in s], "first_sum", after)


def second_sum(info, keep_a, recv_a, keep_b, recv_b, after):
    dim = keep_b.shape[1]
    top, rest = keep_a.shape[0], keep_b.shape[0]
    quarters = lax.axis_size("replica") == REPLICAS
    rows = -(-(top + rest) // (PAD * REPLICAS)) * PAD

    def kernel(info, ka, ra, kb, rb, *refs):
        whole = refs[-1]
        add_rows(whole, 0, ka, ra, 0, top)
        add_rows(whole, top, kb, rb, 0, rest)
        for k in range(REPLICAS if quarters else 0):
            owner = (info[3] + k) % REPLICAS

            @pl.loop(0, rows // PAD)
            def _(i):
                src = pl.ds(pl.multiple_of(owner * rows + i * PAD, PAD), PAD)
                refs[k][pl.ds(pl.multiple_of(i * PAD, PAD), PAD), :] = whole[src, :]

    ins = [info, keep_a, recv_a, keep_b, recv_b]
    if quarters:
        outs = [shape((rows, dim), BF)] * REPLICAS
        scratch = [pltpu.VMEM((REPLICAS * rows, dim), BF)]
    else:
        outs, scratch = [shape((top + rest, dim), BF)], []
    return vmem_call(kernel, outs, ins, "second_sum", after, scratch)


def quarter_sum(parts, after):
    rows, dim = parts[0].shape

    def kernel(*refs):
        out = refs[-1]

        @pl.loop(0, rows // PAD)
        def _(i):
            at = pl.ds(pl.multiple_of(i * PAD, PAD), PAD)
            total = refs[0][at, :].astype(F32)
            for ref in refs[1:-1]:
                total = total + ref[at, :].astype(F32)
            out[at, :] = total.astype(BF)

    return vmem_call(kernel, [shape((rows, dim), BF)], list(parts), "quarter_sum", after)[0]


def own_pieces(row, count, width, group):
    share = count * width // GROUPS
    at, pieces = group * share, []
    while at < (group + 1) * share:
        size = min((group + 1) * share - at, width - at % width)
        pieces.append((row + at // width, at % width, size, at - group * share))
        at += size
    return pieces


def finish(info, quarters, kind, after):
    dim = quarters[0].shape[1]
    share = dim // GROUPS
    half = 3 * share // 2
    vectors = ((ROW_QKV, 3), (ROW_OUT, 1), (ROW_UP, 4), (ROW_DOWN, 1))
    if kind == "mlp":
        outs = [shape((dim, dim), F32), shape((share, 4 * dim), F32), shape((share, dim), F32)]
    else:
        outs = [shape((share, 3 * dim), F32)]
    large = len(outs)
    if kind == "qkv":
        outs += [shape((1, count * dim // GROUPS), F32) for _, count in vectors]
        outs += [shape((2, share), F32)] * 2
    rows = quarters[0].shape[0]

    def kernel(info, *refs):
        given, refs = refs[: len(quarters)], refs[len(quarters) :]
        out_h = refs[:large]
        small = refs[large : len(outs)]
        src = refs[len(outs)]
        stage = refs[len(outs) + 1 : -1]
        sems = refs[-1]
        for owner in range(len(quarters)):
            dst, sem = src.at[pl.ds(owner * rows, rows)], sems.at[owner]
            for k in range(len(quarters)):
                here = (info[3] - owner + REPLICAS) % REPLICAS == k

                @pl.when(here if len(quarters) > 1 else info[3] >= 0)
                def _():
                    pltpu.make_async_copy(given[k], dst, sem).start()

        for owner in range(len(quarters)):
            dst, sem = src.at[pl.ds(owner * rows, rows)], sems.at[owner]
            pltpu.make_async_copy(given[0], dst, sem).wait()
        if kind == "mlp":
            stage[0][...] = src[:dim, :].astype(F32)
            for i in range(4):
                block = src[dim + i * share : dim + (i + 1) * share, :].astype(F32)
                stage[1][:, i * dim : (i + 1) * dim] = block
            stage[2][...] = src[dim + 4 * share : dim + 5 * share, :].astype(F32)
        else:
            for i in range(3):
                at, left, to = i * share, share, 0
                while left:
                    count = min(left, half - at % half)
                    row = at if at < half else at + PAD
                    block = src[row : row + count, :].astype(F32)
                    stage[0][to : to + count, i * dim : (i + 1) * dim] = block
                    at, left, to = at + count, left - count, to + count
        copies = [
            pltpu.make_async_copy(s, o, sems.at[REPLICAS + i])
            for i, (s, o) in enumerate(zip(stage, out_h))
        ]
        for copy in copies:
            copy.start()
        if kind == "qkv":
            tail = src[half : half + PAD, :].astype(F32)
            for group in range(GROUPS):

                @pl.when(info[1] + 2 * info[2] == group)
                def _():
                    for out, (row, count) in zip(small, vectors):
                        for r, c, size, at in own_pieces(row, count, dim, group):
                            out[:, at : at + size] = tail[r : r + 1, c : c + size]
                    for out, row in zip(small[4:], (ROW_GAIN, ROW_SHIFT)):
                        out[...] = tail[row : row + 2, group * share : (group + 1) * share]

        for copy in copies:
            copy.wait()

    scratch = [pltpu.VMEM((len(quarters) * rows, dim), BF)] + [vmem_like(o) for o in outs[:large]]
    places = "h" * large + "v" * (len(outs) - large)
    ins = [info] + list(quarters)
    return call(
        kernel, outs, ins, scratch, 8, {}, "finish", after, 14, "s" + "a" * len(quarters), places
    )


def flow(shard, axis, pairs, sections):
    if sections == (0, 1):
        return lax.ppermute(shard, axis, pairs)
    peers = lax.axis_size(axis)
    pairs = [(s * peers + i, s * peers + j) for s in sections for i, j in pairs]
    return lax.ppermute(shard, ("section", axis), pairs)


ACROSS = [(g, g ^ 1) for g in range(GROUPS)]
ALONG = [(g, g ^ 2) for g in range(GROUPS)]
BOTH = (0, 1)


def exchange(a, b, turned, sections):
    ways = (ALONG, ACROSS) if turned else (ACROSS, ALONG)
    return flow(a, "group", ways[0], sections), flow(b, "group", ways[1], sections)


def replica_send(parts):
    if len(parts) == 1:
        return [lax.psum(parts[0], "replica")]
    return [shift(part, k) if k else part for k, part in enumerate(parts)]


def shift(part, by):
    pairs = [(i, (i + by) % REPLICAS) for i in range(REPLICAS)]
    return lax.ppermute(part, "replica", pairs)


def replica_sum(parts, after):
    if len(parts) == 1:
        return parts
    own = quarter_sum(parts, after)
    return [own] + [shift(own, k) for k in range(1, REPLICAS)]


def shards(
    block_input,
    cotangent,
    crop_count,
    mask_count,
    qkv_weight,
    qkv_bias,
    out_weight,
    out_bias,
    up_weight,
    up_bias,
    down_weight,
    down_bias,
    norm_gain,
    norm_shift,
):
    params = (
        qkv_weight[0],
        qkv_bias,
        out_weight[0],
        out_bias,
        up_weight[0],
        up_bias,
        down_weight[0],
        down_bias,
        norm_gain[0],
        norm_shift[0],
    )
    rows, dim = block_input.shape
    tab = jnp.asarray(rotary_tables())
    tab_t = jnp.asarray(rotary_columns())
    group = lax.axis_index("group")
    assert lax.axis_size("group") == GROUPS
    info = jnp.stack([lax.axis_index("section"), group % 2, group // 2, lax.axis_index("replica")])

    def to_other(shard, pairs):
        return lax.ppermute(shard, "section", pairs)

    act, first = forward(0, info, crop_count, block_input, None, params, tab, None)
    arrived = [to_other(first[0], [(0, 1)])]
    act, second = forward(1, info, crop_count, block_input, arrived[0], params, tab, act)
    arrived.append(to_other(second[0], [(0, 1)]))
    act, third = forward(2, info, crop_count, block_input, arrived[1], params, tab, act)
    kept_one, kept_zero = (second, third), (first, second)

    common = (info, crop_count, mask_count)
    one, gmid, small, last = mlp_grad(1, *common, cotangent, kept_one, params, None)
    came_one = exchange(one[0], one[2], False, (1,))
    dx, kept, last = attention_grad(
        1, info, gmid, small, arrived, kept_one, params, tab_t, None, last
    )
    grad_back = to_other(dx, [(1, 0)])
    third, last = qkv_grad(1, info, kept, None, last)
    zero, gmid, small, last = mlp_grad(0, *common, grad_back, kept_zero, params, last)
    came_zero = exchange(zero[0], zero[2], False, (0,))
    dx, kept, last = attention_grad(
        0, info, gmid, small, [block_input], kept_zero, params, tab_t, dx, last
    )
    third, last = qkv_grad(0, info, kept, third, last)
    came = exchange(third[0], third[2], False, BOTH)

    sets = [(s[1], c[0], s[3], c[1]) for s, c in ((zero, came_zero), (one, came_one))]
    first_mlp = first_sum(info, sets, last)
    came_mlp = exchange(first_mlp[0], first_mlp[2], True, BOTH)
    first_qkv = first_sum(info, [(third[1], came[0], third[3], came[1])], first_mlp[1])
    came_qkv = exchange(first_qkv[0], first_qkv[2], True, BOTH)
    mlp = second_sum(info, first_mlp[1], came_mlp[0], first_mlp[3], came_mlp[1], first_qkv[1])
    last = mlp[0]
    mlp = replica_send(mlp)
    qkv = second_sum(info, first_qkv[1], came_qkv[0], first_qkv[3], came_qkv[1], last)
    last = qkv[0]
    qkv = replica_send(qkv)
    mlp = replica_sum(mlp, last)
    qkv = replica_sum(qkv, mlp[0])
    grad_down, grad_up, grad_out = finish(info, mlp, "mlp", qkv[0])
    grad_qkv, *small = finish(info, qkv, "qkv", grad_out)
    qkv_b, out_b, up_b, down_b, gain, shift = small
    return (
        act[None],
        dx[None],
        grad_qkv[None],
        qkv_b,
        grad_out[None],
        out_b,
        grad_up[None],
        up_b,
        grad_down[None],
        down_b,
        gain[None],
        shift[None],
    )


def solution(mesh):
    rows = P(("group", "replica"))
    stack = P("section")
    return jax.shard_map(
        shards,
        mesh=mesh,
        in_specs=(rows,) * 4 + (stack,) * 10,
        out_specs=(
            P("section", ("group", "replica"), None),
            P("section", ("group", "replica"), None),
            P("section", "group", None),
            P("section", "group"),
            P("section", "group", None),
            P("section", "group"),
            P("section", "group", None),
            P("section", "group"),
            P("section", "group", None),
            P("section", "group"),
            P("section", None, "group"),
            P("section", None, "group"),
        ),
        check_vma=False,
    )
```

profile of v0, /device:TPU:0, one launch (start us, length us, event | category | flops | bytes accessed | tf_op | source)
XLA Modules:
  0.0 277.8 jit_solution(15734862444510322605)
XLA Ops:
  1.5 11.7 %layer_forward.3 = (bf16[512,640]{1,0:T(8,128)(2,1)}, bf16[256,640]{1,0:T(8,128)(2,1)S(1)}, bf16[256,1920]{1,0:T(8,128)(2,1)S(1)}, bf16[20,256,256]{2,1,0:T(8,12...) custom-call(s32[4]{0:T(128)S(1)} %pad_add_fusion.info.refs_0_, ...), custom_call_target="tpu_custom_call" | custom-call | flops 115000000 | tf_op jit(solution)/shard_map/layer_forward/pallas_call | solution.py:128
  16.6 9.4 %layer_forward.4 = (bf16[512,640]{1,0:T(8,128)(2,1)}, bf16[256,640]{1,0:T(8,128)(2,1)S(1)}, bf16[256,1920]{1,0:T(8,128)(2,1)S(1)}, bf16[20,256,256]{2,1,0:T(8,12...) custom-call(s32[4]{0:T(128)S(1)} %pad_add_fusion.info.refs_0_, ...), custom_call_target="tpu_custom_call", output_to_operand_aliasing={{0}: (15, {})} | custom-call | flops 115000000 | tf_op jit(solution)/shard_map/layer_forward/pallas_call | solution.py:128
  29.6 11.6 %layer_forward.5 = (bf16[512,640]{1,0:T(8,128)(2,1)}, bf16[256,640]{1,0:T(8,128)(2,1)}, bf16[256,1920]{1,0:T(8,128)(2,1)S(1)}, bf16[20,256,256]{2,1,0:T(8,128)(2...) custom-call(s32[4]{0:T(128)S(1)} %pad_add_fusion.info.refs_0_, ...), custom_call_target="tpu_custom_call", output_to_operand_aliasing={{0}: (14, {})} | custom-call | flops 115000000 | tf_op jit(solution)/shard_map/layer_forward/pallas_call | solution.py:128
  43.8 4.4 %attention_grad.2 = (bf16[512,640]{1,0:T(8,128)(2,1)}, bf16[512,1920]{1,0:T(8,128)(2,1)S(1)}, bf16[640,512]{1,0:T(8,128)(2,1)S(1)}, f32[16,640]{1,0:T(8,128)S(1)}, f32[8,128]{1,0:T(8,128)S(1)}) custom-call(s32[4]{0:T(128)S(1)} %pad_add_fusion.info.refs_0_, f32[512,640]{1,0:T(8,128)S(1)} %get-tuple-element.108.refs_1_, bf16[640,640]{1,0:T(8,128)(2,1)S(1)} %bitcast.36, ...), custom_call_target="tpu_custom_call" | custom-call | flops 13799999488 | tf_op jit(solution)/shard_map/attention_grad/pallas_call | solution.py:128
  51.1 29.3 %collective-permute-done.2.refs_3_ = bf16[512,640]{1,0:T(8,128)(2,1)S(1)} collective-permute-done((bf16[512,640]{1,0:T(8,128)(2,1)}, bf16[512,640]{1,0:T(8,128)(2,1)S(1)}, u32[]{:S(2)}, u32[]{:S(2)}) %collective-permute-start.2) | collective-permute-done | bytes 655392 | tf_op jit(solution)/shard_map/ppermute | solution.py:808
  81.8 15.0 %mlp_grad.3 = (bf16[1280,640]{1,0:T(8,128)(2,1)}, bf16[1280,640]{1,0:T(8,128)(2,1)S(1)}, bf16[1600,640]{1,0:T(8,128)(2,1)}, bf16[1600,640]{1,0:T(8,128)(2,1)S(1)...) custom-call(s32[4]{0:T(128)S(1)} %pad_add_fusion.info.refs_0_, s32[1]{0:T(128)S(6)} %copy.42.live.refs_1_, ...), custom_call_target="tpu_custom_call" | custom-call | flops 11500000256 | tf_op jit(solution)/shard_map/mlp_grad/pallas_call | solution.py:128
  96.7 4.9 %collective-permute-start.6 = (bf16[1600,640]{1,0:T(8,128)(2,1)}, bf16[1600,640]{1,0:T(8,128)(2,1)S(1)}, u32[]{:S(2)}, u32[]{:S(2)}) collective-permute-start(bf16[1600,640]{1,0:T(8,128)(2,1)} %get-tuple-element.146), channel_id=1, source_target_pairs={{0,8},{4,12},{8,0},{12,4},{1,9},{5,13},{9,1},{13,5},{2,10},{6,14},... | collective-permute-start | bytes 6144008 | tf_op jit(solution)/shard_map/ppermute | solution.py:741
  102.4 3.4 %collective-permute-start.5 = (bf16[1280,640]{1,0:T(8,128)(2,1)}, bf16[1280,640]{1,0:T(8,128)(2,1)S(1)}, u32[]{:S(2)}, u32[]{:S(2)}) collective-permute-start(bf16[1280,640]{1,0:T(8,128)(2,1)} %get-tuple-element.144), channel_id=1, source_target_pairs={{0,4},{4,0},{8,12},{12,8},{1,5},{5,1},{9,13},{13,9},{2,6},{6,2},{1... | collective-permute-start | bytes 4915208 | tf_op jit(solution)/shard_map/ppermute | solution.py:741
  105.8 12.6 %attention_grad.3 = (bf16[512,640]{1,0:T(8,128)(2,1)}, bf16[512,1920]{1,0:T(8,128)(2,1)S(1)}, bf16[640,512]{1,0:T(8,128)(2,1)S(1)}, f32[16,640]{1,0:T(8,128)S(1)}, f32[8,128]{1,0:T(8,128)S(1)}) custom-call(s32[4]{0:T(128)S(1)} %pad_add_fusion.info.refs_0_, f32[512,640]{1,0:T(8,128)S(1)} %get-tuple-element.125.refs_1_, ...), custom_call_target="tpu_custom_call", output_to_operand_aliasing={{0}: (15, {})} | custom-call | flops 13799999488 | tf_op jit(solution)/shard_map/attention_grad/pallas_call | solution.py:128
  118.5 2.9 %qkv_grad.3 = (bf16[496,640]{1,0:T(8,128)(2,1)S(1)}, bf16[496,640]{1,0:T(8,128)(2,1)S(1)}, bf16[480,640]{1,0:T(8,128)(2,1)S(1)}, bf16[480,640]{1,0:T(8,128)(2,1)S(1)}, f32[8,128]{1,0:T(8,128)S(1)}) custom-call(s32[4]{0:T(128)S(1)} %pad_add_fusion.info.refs_0_, ...), custom_call_target="tpu_custom_call", output_to_operand_aliasing={{0}: (4, {}), {1}: (5, {}), {2}: (6, {}), {3}: (7, {})} | custom-call | flops 115000000 | tf_op jit(solution)/shard_map/qkv_grad/pallas_call | solution.py:128
  121.4 17.4 %collective-permute-done.5.refs_2_ = bf16[1280,640]{1,0:T(8,128)(2,1)S(1)} collective-permute-done((bf16[1280,640]{1,0:T(8,128)(2,1)}, bf16[1280,640]{1,0:T(8,128)(2,1)S(1)}, u32[]{:S(2)}, u32[]{:S(2)}) %collective-permute-start.5) | collective-permute-done | bytes 1638432 | tf_op jit(solution)/shard_map/ppermute | solution.py:741
  144.5 16.4 %collective-permute-done.4.refs_4_ = bf16[480,640]{1,0:T(8,128)(2,1)S(1)} collective-permute-done((bf16[480,640]{1,0:T(8,128)(2,1)S(1)}, bf16[480,640]{1,0:T(8,128)(2,1)S(1)}, u32[]{:S(2)}, u32[]{:S(2)}) %collective-permute-start.4) | collective-permute-done | bytes 614432 | tf_op jit(solution)/shard_map/ppermute | solution.py:738
  160.9 8.4 %collective-permute-done.3.refs_2_ = bf16[496,640]{1,0:T(8,128)(2,1)S(1)} collective-permute-done((bf16[496,640]{1,0:T(8,128)(2,1)S(1)}, bf16[496,640]{1,0:T(8,128)(2,1)S(1)}, u32[]{:S(2)}, u32[]{:S(2)}) %collective-permute-start.3) | collective-permute-done | bytes 634912 | tf_op jit(solution)/shard_map/ppermute | solution.py:738
  179.9 5.4 %collective-permute-done.10.refs_4_ = bf16[240,640]{1,0:T(8,128)(2,1)S(1)} collective-permute-done((bf16[240,640]{1,0:T(8,128)(2,1)S(1)}, bf16[240,640]{1,0:T(8,128)(2,1)S(1)}, u32[]{:S(2)}, u32[]{:S(2)}) %collective-permute-start.10) | collective-permute-done | bytes 307232 | tf_op jit(solution)/shard_map/ppermute | solution.py:738
  186.3 9.6 %collective-permute-done.17.refs_2_ = bf16[368,640]{1,0:T(8,128)(2,1)S(1)} collective-permute-done((bf16[368,640]{1,0:T(8,128)(2,1)S(1)}, bf16[368,640]{1,0:T(8,128)(2,1)S(1)}, u32[]{:S(2)}, u32[]{:S(2)}) %collective-permute-start.17) | collective-permute-done | bytes 471072 | tf_op jit(solution)/shard_map/ppermute | solution.py:762
  196.3 19.8 %collective-permute-start.24 = (bf16[368,640]{1,0:T(8,128)(2,1)S(1)}, bf16[368,640]{1,0:T(8,128)(2,1)S(1)}, u32[]{:S(2)}, u32[]{:S(2)}) collective-permute-start(bf16[368,640]{1,0:T(8,128)(2,1)S(1)} %quarter_sum.2.refs_4_.refs_1_), channel_id=1, source_target_pairs={{0,3},{1,0},{2,1},{3,2},{4,7},{5,4},{6,5},{7,6},{8,11},{9,8},{10,9... | collective-permute-start | bytes 1413128 | tf_op jit(solution)/shard_map/ppermute | solution.py:762
  216.2 3.6 %collective-permute-start.13 = (bf16[128,640]{1,0:T(8,128)(2,1)S(1)}, bf16[128,640]{1,0:T(8,128)(2,1)S(1)}, u32[]{:S(2)}, u32[]{:S(2)}) collective-permute-start(bf16[128,640]{1,0:T(8,128)(2,1)S(1)} %get-tuple-element.162), channel_id=1, source_target_pairs={{0,1},{1,2},{2,3},{3,0},{4,5},{5,6},{6,7},{7,4},{8,9},{9,10},{10,1... | collective-permute-start | bytes 491528 | tf_op jit(solution)/shard_map/ppermute | solution.py:762
  221.7 2.9 %collective-permute-start.14 = (bf16[128,640]{1,0:T(8,128)(2,1)S(1)}, bf16[128,640]{1,0:T(8,128)(2,1)S(1)}, u32[]{:S(2)}, u32[]{:S(2)}) collective-permute-start(bf16[128,640]{1,0:T(8,128)(2,1)S(1)} %get-tuple-element.163), channel_id=1, source_target_pairs={{0,2},{1,3},{2,0},{3,1},{4,6},{5,7},{6,4},{7,5},{8,10},{9,11},{10,... | collective-permute-start | bytes 491528 | tf_op jit(solution)/shard_map/ppermute | solution.py:762
  224.7 4.0 %collective-permute-done.13.refs_1_ = bf16[128,640]{1,0:T(8,128)(2,1)S(1)} collective-permute-done((bf16[128,640]{1,0:T(8,128)(2,1)S(1)}, bf16[128,640]{1,0:T(8,128)(2,1)S(1)}, u32[]{:S(2)}, u32[]{:S(2)}) %collective-permute-start.13) | collective-permute-done | bytes 163872 | tf_op jit(solution)/shard_map/ppermute | solution.py:762
  229.3 30.5 %collective-permute-done.14.refs_2_ = bf16[128,640]{1,0:T(8,128)(2,1)S(1)} collective-permute-done((bf16[128,640]{1,0:T(8,128)(2,1)S(1)}, bf16[128,640]{1,0:T(8,128)(2,1)S(1)}, u32[]{:S(2)}, u32[]{:S(2)}) %collective-permute-start.14) | collective-permute-done | bytes 163872 | tf_op jit(solution)/shard_map/ppermute | solution.py:762
  259.9 2.7 collective-permute-start.21
  264.7 3.9 %finish.2 = (f32[640,640]{1,0:T(8,128)}, f32[160,2560]{1,0:T(8,128)}, f32[160,640]{1,0:T(8,128)}) custom-call(s32[4]{0:T(128)S(1)} %pad_add_fusion.info.refs_0_, bf16[368,640]{1,0:T(8,128)(2,1)S(1)} %quarter_sum.2.refs_4_.refs_1_, bf16[368,640]{1,0:T(8,128)(2,1)S(1)} %collective-permute-done.22.refs_2_, ...), custom_call_target="tpu_custom_call" | custom-call | flops 115000000 | tf_op jit(solution)/shard_map/finish/pallas_call | solution.py:128
  268.6 4.6 %collective-permute-done.20.refs_3_ = bf16[128,640]{1,0:T(8,128)(2,1)S(1)} collective-permute-done((bf16[128,640]{1,0:T(8,128)(2,1)S(1)}, bf16[128,640]{1,0:T(8,128)(2,1)S(1)}, u32[]{:S(2)}, u32[]{:S(2)}) %collective-permute-start.20) | collective-permute-done | bytes 163872 | tf_op jit(solution)/shard_map/ppermute | solution.py:762
  274.2 3.4 %finish.3 = (f32[160,1920]{1,0:T(8,128)}, f32[1,480]{1,0:T(1,128)}, f32[1,160]{1,0:T(1,128)}, f32[1,640]{1,0:T(1,128)}, f32[1,160]{1,0:T(1,128)}, /*index=5*/f32[2,160]{1,0:T(2,128)}, f32[2,160]{1,0:T(2,128)}) custom-call(s32[4]{0:T(128)S(1)} %pad_add_fusion.info.refs_0_, bf16[128,640]{1,0:T(8,128)(2,1)S(1)} %quarter_sum.3.refs_5_.refs_1_, ...), custom_call_target="tpu_custom_call" | custom-call | flops 115000000 | tf_op jit(solution)/shard_map/finish/pallas_call | solution.py:128
  (108 shorter events, 38.0 us)
Async XLA Ops:
  26.1 3.5 %collective-permute-start.1 = (bf16[256,640]{1,0:T(8,128)(2,1)S(1)}, bf16[256,640]{1,0:T(8,128)(2,1)S(1)}, u32[]{:S(2)}, u32[]{:S(2)}) collective-permute-start(bf16[256,640]{1,0:T(8,128)(2,1)S(1)} %get-tuple-element.97), channel_id=1, source_target_pairs={{0,16},{1,17},{2,18},{3,19},{4,20},{5,21},{6,22},{7,23},{8,24},{9,... | collective-permute-start | bytes 983048 | tf_op jit(solution)/shard_map/ppermute | solution.py:808
  48.2 32.2 %collective-permute-start.2 = (bf16[512,640]{1,0:T(8,128)(2,1)}, bf16[512,640]{1,0:T(8,128)(2,1)S(1)}, u32[]{:S(2)}, u32[]{:S(2)}) collective-permute-start(bf16[512,640]{1,0:T(8,128)(2,1)} %get-tuple-element.115.refs_15_), channel_id=1, source_target_pairs={{16,0},{17,1},{18,2},{19,3},{20,4},{21,5},{22,6},{23,7},{24,8},{25... | collective-permute-start | bytes 1966088 | tf_op jit(solution)/shard_map/ppermute | solution.py:808
  49.7 71.6 %collective-permute-start.8 = (bf16[1600,640]{1,0:T(8,128)(2,1)}, bf16[1600,640]{1,0:T(8,128)(2,1)S(1)}, u32[]{:S(2)}, u32[]{:S(2)}) collective-permute-start(bf16[1600,640]{1,0:T(8,128)(2,1)} %get-tuple-element.150), channel_id=1, source_target_pairs={{16,24},{20,28},{24,16},{28,20},{17,25},{21,29},{25,17},{29,21},{1... | collective-permute-start | bytes 6144008 | tf_op jit(solution)/shard_map/ppermute | solution.py:741
  96.7 42.0 %collective-permute-start.6 = (bf16[1600,640]{1,0:T(8,128)(2,1)}, bf16[1600,640]{1,0:T(8,128)(2,1)S(1)}, u32[]{:S(2)}, u32[]{:S(2)}) collective-permute-start(bf16[1600,640]{1,0:T(8,128)(2,1)} %get-tuple-element.146), channel_id=1, source_target_pairs={{0,8},{4,12},{8,0},{12,4},{1,9},{5,13},{9,1},{13,5},{2,10},{6,14},... | collective-permute-start | bytes 6144008 | tf_op jit(solution)/shard_map/ppermute | solution.py:741
  101.6 19.7 %collective-permute-start.7 = (bf16[1280,640]{1,0:T(8,128)(2,1)}, bf16[1280,640]{1,0:T(8,128)(2,1)S(1)}, u32[]{:S(2)}, u32[]{:S(2)}) collective-permute-start(bf16[1280,640]{1,0:T(8,128)(2,1)} %get-tuple-element.148), channel_id=1, source_target_pairs={{16,20},{20,16},{24,28},{28,24},{17,21},{21,17},{25,29},{29,25},{1... | collective-permute-start | bytes 4915208 | tf_op jit(solution)/shard_map/ppermute | solution.py:741
  102.4 36.3 %collective-permute-start.5 = (bf16[1280,640]{1,0:T(8,128)(2,1)}, bf16[1280,640]{1,0:T(8,128)(2,1)S(1)}, u32[]{:S(2)}, u32[]{:S(2)}) collective-permute-start(bf16[1280,640]{1,0:T(8,128)(2,1)} %get-tuple-element.144), channel_id=1, source_target_pairs={{0,4},{4,0},{8,12},{12,8},{1,5},{5,1},{9,13},{13,9},{2,6},{6,2},{1... | collective-permute-start | bytes 4915208 | tf_op jit(solution)/shard_map/ppermute | solution.py:741
  140.4 29.8 %collective-permute-start.12 = (bf16[800,640]{1,0:T(8,128)(2,1)S(1)}, bf16[800,640]{1,0:T(8,128)(2,1)S(1)}, u32[]{:S(2)}, u32[]{:S(2)}) collective-permute-start(bf16[800,640]{1,0:T(8,128)(2,1)S(1)} %get-tuple-element.159), channel_id=1, source_target_pairs={{0,4},{4,0},{8,12},{12,8},{1,5},{5,1},{9,13},{13,9},{2,6},{6,2},{1... | collective-permute-start | bytes 3072008 | tf_op jit(solution)/shard_map/ppermute | solution.py:738
  141.9 28.3 %collective-permute-start.11 = (bf16[640,640]{1,0:T(8,128)(2,1)S(1)}, bf16[640,640]{1,0:T(8,128)(2,1)S(1)}, u32[]{:S(2)}, u32[]{:S(2)}) collective-permute-start(bf16[640,640]{1,0:T(8,128)(2,1)S(1)} %get-tuple-element.157), channel_id=1, source_target_pairs={{0,8},{4,12},{8,0},{12,4},{1,9},{5,13},{9,1},{13,5},{2,10},{6,14},... | collective-permute-start | bytes 2457608 | tf_op jit(solution)/shard_map/ppermute | solution.py:738
  142.4 26.8 %collective-permute-start.3 = (bf16[496,640]{1,0:T(8,128)(2,1)S(1)}, bf16[496,640]{1,0:T(8,128)(2,1)S(1)}, u32[]{:S(2)}, u32[]{:S(2)}) collective-permute-start(bf16[496,640]{1,0:T(8,128)(2,1)S(1)} %get-tuple-element.140), channel_id=1, source_target_pairs={{0,4},{4,0},{8,12},{12,8},{1,5},{5,1},{9,13},{13,9},{2,6},{6,2},{1... | collective-permute-start | bytes 1904648 | tf_op jit(solution)/shard_map/ppermute | solution.py:738
  142.5 18.3 %collective-permute-start.4 = (bf16[480,640]{1,0:T(8,128)(2,1)S(1)}, bf16[480,640]{1,0:T(8,128)(2,1)S(1)}, u32[]{:S(2)}, u32[]{:S(2)}) collective-permute-start(bf16[480,640]{1,0:T(8,128)(2,1)S(1)} %get-tuple-element.142), channel_id=1, source_target_pairs={{0,8},{4,12},{8,0},{12,4},{1,9},{5,13},{9,1},{13,5},{2,10},{6,14},... | collective-permute-start | bytes 1843208 | tf_op jit(solution)/shard_map/ppermute | solution.py:738
  171.9 14.4 %collective-permute-start.16 = (bf16[368,640]{1,0:T(8,128)(2,1)S(1)}, bf16[368,640]{1,0:T(8,128)(2,1)S(1)}, u32[]{:S(2)}, u32[]{:S(2)}) collective-permute-start(bf16[368,640]{1,0:T(8,128)(2,1)S(1)} %get-tuple-element.165), channel_id=1, source_target_pairs={{0,1},{1,2},{2,3},{3,0},{4,5},{5,6},{6,7},{7,4},{8,9},{9,10},{10,1... | collective-permute-start | bytes 1413128 | tf_op jit(solution)/shard_map/ppermute | solution.py:762
  174.0 21.9 %collective-permute-start.17 = (bf16[368,640]{1,0:T(8,128)(2,1)S(1)}, bf16[368,640]{1,0:T(8,128)(2,1)S(1)}, u32[]{:S(2)}, u32[]{:S(2)}) collective-permute-start(bf16[368,640]{1,0:T(8,128)(2,1)S(1)} %get-tuple-element.166), channel_id=1, source_target_pairs={{0,2},{1,3},{2,0},{3,1},{4,6},{5,7},{6,4},{7,5},{8,10},{9,11},{10,... | collective-permute-start | bytes 1413128 | tf_op jit(solution)/shard_map/ppermute | solution.py:762
  176.6 19.3 %collective-permute-start.18 = (bf16[368,640]{1,0:T(8,128)(2,1)S(1)}, bf16[368,640]{1,0:T(8,128)(2,1)S(1)}, u32[]{:S(2)}, u32[]{:S(2)}) collective-permute-start(bf16[368,640]{1,0:T(8,128)(2,1)S(1)} %get-tuple-element.167), channel_id=1, source_target_pairs={{0,3},{1,0},{2,1},{3,2},{4,7},{5,4},{6,5},{7,6},{8,11},{9,8},{10,9... | collective-permute-start | bytes 1413128 | tf_op jit(solution)/shard_map/ppermute | solution.py:762
  177.9 7.4 %collective-permute-start.9 = (bf16[256,640]{1,0:T(8,128)(2,1)S(1)}, bf16[256,640]{1,0:T(8,128)(2,1)S(1)}, u32[]{:S(2)}, u32[]{:S(2)}) collective-permute-start(bf16[256,640]{1,0:T(8,128)(2,1)S(1)} %get-tuple-element.154), channel_id=1, source_target_pairs={{0,8},{4,12},{8,0},{12,4},{1,9},{5,13},{9,1},{13,5},{2,10},{6,14},... | collective-permute-start | bytes 983048 | tf_op jit(solution)/shard_map/ppermute | solution.py:738
  178.4 6.9 %collective-permute-start.10 = (bf16[240,640]{1,0:T(8,128)(2,1)S(1)}, bf16[240,640]{1,0:T(8,128)(2,1)S(1)}, u32[]{:S(2)}, u32[]{:S(2)}) collective-permute-start(bf16[240,640]{1,0:T(8,128)(2,1)S(1)} %get-tuple-element.156), channel_id=1, source_target_pairs={{0,4},{4,0},{8,12},{12,8},{1,5},{5,1},{9,13},{13,9},{2,6},{6,2},{1... | collective-permute-start | bytes 921608 | tf_op jit(solution)/shard_map/ppermute | solution.py:738
  196.3 68.3 %collective-permute-start.24 = (bf16[368,640]{1,0:T(8,128)(2,1)S(1)}, bf16[368,640]{1,0:T(8,128)(2,1)S(1)}, u32[]{:S(2)}, u32[]{:S(2)}) collective-permute-start(bf16[368,640]{1,0:T(8,128)(2,1)S(1)} %quarter_sum.2.refs_4_.refs_1_), channel_id=1, source_target_pairs={{0,3},{1,0},{2,1},{3,2},{4,7},{5,4},{6,5},{7,6},{8,11},{9,8},{10,9... | collective-permute-start | bytes 1413128 | tf_op jit(solution)/shard_map/ppermute | solution.py:762
  216.2 12.5 %collective-permute-start.13 = (bf16[128,640]{1,0:T(8,128)(2,1)S(1)}, bf16[128,640]{1,0:T(8,128)(2,1)S(1)}, u32[]{:S(2)}, u32[]{:S(2)}) collective-permute-start(bf16[128,640]{1,0:T(8,128)(2,1)S(1)} %get-tuple-element.162), channel_id=1, source_target_pairs={{0,1},{1,2},{2,3},{3,0},{4,5},{5,6},{6,7},{7,4},{8,9},{9,10},{10,1... | collective-permute-start | bytes 491528 | tf_op jit(solution)/shard_map/ppermute | solution.py:762
  219.8 44.9 %collective-permute-start.23 = (bf16[368,640]{1,0:T(8,128)(2,1)S(1)}, bf16[368,640]{1,0:T(8,128)(2,1)S(1)}, u32[]{:S(2)}, u32[]{:S(2)}) collective-permute-start(bf16[368,640]{1,0:T(8,128)(2,1)S(1)} %quarter_sum.2.refs_4_.refs_1_), channel_id=1, source_target_pairs={{0,2},{1,3},{2,0},{3,1},{4,6},{5,7},{6,4},{7,5},{8,10},{9,11},{10,... | collective-permute-start | bytes 1413128 | tf_op jit(solution)/shard_map/ppermute | solution.py:762
  221.2 43.5 %collective-permute-start.22 = (bf16[368,640]{1,0:T(8,128)(2,1)S(1)}, bf16[368,640]{1,0:T(8,128)(2,1)S(1)}, u32[]{:S(2)}, u32[]{:S(2)}) collective-permute-start(bf16[368,640]{1,0:T(8,128)(2,1)S(1)} %quarter_sum.2.refs_4_.refs_1_), channel_id=1, source_target_pairs={{0,1},{1,2},{2,3},{3,0},{4,5},{5,6},{6,7},{7,4},{8,9},{9,10},{10,1... | collective-permute-start | bytes 1413128 | tf_op jit(solution)/shard_map/ppermute | solution.py:762
  221.7 38.1 %collective-permute-start.14 = (bf16[128,640]{1,0:T(8,128)(2,1)S(1)}, bf16[128,640]{1,0:T(8,128)(2,1)S(1)}, u32[]{:S(2)}, u32[]{:S(2)}) collective-permute-start(bf16[128,640]{1,0:T(8,128)(2,1)S(1)} %get-tuple-element.163), channel_id=1, source_target_pairs={{0,2},{1,3},{2,0},{3,1},{4,6},{5,7},{6,4},{7,5},{8,10},{9,11},{10,... | collective-permute-start | bytes 491528 | tf_op jit(solution)/shard_map/ppermute | solution.py:762
  228.6 31.2 %collective-permute-start.15 = (bf16[128,640]{1,0:T(8,128)(2,1)S(1)}, bf16[128,640]{1,0:T(8,128)(2,1)S(1)}, u32[]{:S(2)}, u32[]{:S(2)}) collective-permute-start(bf16[128,640]{1,0:T(8,128)(2,1)S(1)} %get-tuple-element.164), channel_id=1, source_target_pairs={{0,3},{1,0},{2,1},{3,2},{4,7},{5,4},{6,5},{7,6},{8,11},{9,8},{10,9... | collective-permute-start | bytes 491528 | tf_op jit(solution)/shard_map/ppermute | solution.py:762
  259.9 8.7 %collective-permute-start.21 = (bf16[128,640]{1,0:T(8,128)(2,1)S(1)}, bf16[128,640]{1,0:T(8,128)(2,1)S(1)}, u32[]{:S(2)}, u32[]{:S(2)}) collective-permute-start(bf16[128,640]{1,0:T(8,128)(2,1)S(1)} %quarter_sum.3.refs_5_.refs_1_), channel_id=1, source_target_pairs={{0,3},{1,0},{2,1},{3,2},{4,7},{5,4},{6,5},{7,6},{8,11},{9,8},{10,9... | collective-permute-start | bytes 491528 | tf_op jit(solution)/shard_map/ppermute | solution.py:762
  262.6 10.6 %collective-permute-start.20 = (bf16[128,640]{1,0:T(8,128)(2,1)S(1)}, bf16[128,640]{1,0:T(8,128)(2,1)S(1)}, u32[]{:S(2)}, u32[]{:S(2)}) collective-permute-start(bf16[128,640]{1,0:T(8,128)(2,1)S(1)} %quarter_sum.3.refs_5_.refs_1_), channel_id=1, source_target_pairs={{0,2},{1,3},{2,0},{3,1},{4,6},{5,7},{6,4},{7,5},{8,10},{9,11},{10,... | collective-permute-start | bytes 491528 | tf_op jit(solution)/shard_map/ppermute | solution.py:762
  264.7 8.6 %collective-permute-start.19 = (bf16[128,640]{1,0:T(8,128)(2,1)S(1)}, bf16[128,640]{1,0:T(8,128)(2,1)S(1)}, u32[]{:S(2)}, u32[]{:S(2)}) collective-permute-start(bf16[128,640]{1,0:T(8,128)(2,1)S(1)} %quarter_sum.3.refs_5_.refs_1_), channel_id=1, source_target_pairs={{0,1},{1,2},{2,3},{3,0},{4,5},{5,6},{6,7},{7,4},{8,9},{9,10},{10,1... | collective-permute-start | bytes 491528 | tf_op jit(solution)/shard_map/ppermute | solution.py:762
  (33 other events, 534.9 us)
where the time goes:
time: 281 us; the launch traced here: 278 us
  waiting for transfers between devices  128 us (46%)
  Pallas kernels  83.6 us (30%)
  starting transfers between devices  60.8 us (22%)
  local copies, waits for them, and re-layouts  3.2 us (1%)
    pallas_call x17, Pallas kernels, call(): pl.pallas_call(body, out_shape=outs, in_specs=in_specs, out_specs=[places...  83.6 us
    ppermute x12, waiting for transfers between devices, shift(): return lax.ppermute(part, 'replica', pairs)  48.7 us
    ppermute x12, starting transfers between devices, shift(): return lax.ppermute(part, 'replica', pairs)  39.8 us
    ppermute x3, waiting for transfers between devices, to_other(): return lax.ppermute(shard, 'section', pairs)  31.8 us
    ppermute x6, waiting for transfers between devices, flow(): return lax.ppermute(shard, axis, pairs)  30.1 us
    ppermute x4, waiting for transfers between devices, flow(): return lax.ppermute(shard, ('section', axis), pairs)  17.4 us
    ppermute x4, starting transfers between devices, flow(): return lax.ppermute(shard, ('section', axis), pairs)  9.82 us
    ppermute x6, starting transfers between devices, flow(): return lax.ppermute(shard, axis, pairs)  6.11 us
  transfers between devices with their start and end apart: 25, of which 11 were waited for; matrix products, arithmetic and copies ran while one was open for 0% of the time, Pallas kernels for 13%

commit v1 on v0

--- a/solution.py
+++ b/solution.py
@@ -574,75 +574,207 @@
     return call(kernel, outs, ins, list(scratch), 0, {}, name, after, 8)
 
 
-def first_sum(info, sets, after):
-    dim = sets[0][0].shape[1]
-    sizes = [(k.shape[0] // (2 * PAD) * PAD, k.shape[0] % (2 * PAD)) for k in sets[0][::2]]
+def copy_rows(out, at, src, start, count):
+    whole = count // STEP * STEP
+
+    @pl.loop(0, whole // STEP)
+    def _(i):
+        lines = pl.ds(pl.multiple_of(start + i * STEP, PAD), STEP)
+        out[pl.ds(pl.multiple_of(at + i * STEP, PAD), STEP), :] = src[lines, :]
+
+    if count > whole:
+        lines = pl.ds(pl.multiple_of(start + whole, PAD), count - whole)
+        out[pl.ds(pl.multiple_of(at + whole, PAD), count - whole), :] = src[lines, :]
+
+
+def first_sum(info, sets, third, after):
+    dim = third[0].shape[1]
+    halves = [k.shape[0] // 2 for k in sets[0][::2]]
+    riders = (third[2], third[0])
 
     def kernel(info, *refs):
-        sa, na, sb, nb = refs[4 * len(sets) :]
+        given = refs[4 * len(sets) : 4 * len(sets) + 2]
+        sa, na, sb, nb = refs[4 * len(sets) + 2 :]
+        for out, half, rider in ((sa, halves[0], given[0]), (sb, halves[1], given[1])):
+            copy_rows(out, half, rider, 0, rider.shape[0])
         for section in range(len(sets)):
             ka, ra, kb, rb = refs[4 * section : 4 * section + 4]
-            active = info[0] == section if len(sets) > 1 else info[0] >= 0
-
-            @pl.when(active)
+
+            @pl.when(info[0] == section)
             def _():
-                for own, one, two, new, out, (half, extra) in (
-                    (info[2], ka, ra, na, sa, sizes[0]),
-                    (info[1], kb, rb, nb, sb, sizes[1]),
+                for own, one, two, new, out, half in (
+                    (info[2], ka, ra, na, sa, halves[0]),
+                    (info[1], kb, rb, nb, sb, halves[1]),
                 ):
                     add_rows(out, 0, one, two, (1 - own) * half, half)
                     add_rows(new, 0, one, two, own * half, half)
-                    if extra:
-                        tail = plus(one[2 * half :, :], two[2 * half :, :])
-                        new[half:, :] = tail
-                        out[half:, :] = tail
-
-    outs = [shape((sum(size), dim), BF) for size in sizes for _ in range(2)]
-    return vmem_call(kernel, outs, [info] + [a for s in sets for a in s], "first_sum", after)
-
-
-def second_sum(info, keep_a, recv_a, keep_b, recv_b, after):
-    dim = keep_b.shape[1]
-    top, rest = keep_a.shape[0], keep_b.shape[0]
-    quarters = lax.axis_size("replica") == REPLICAS
-    rows = -(-(top + rest) // (PAD * REPLICAS)) * PAD
-
-    def kernel(info, ka, ra, kb, rb, *refs):
-        whole = refs[-1]
-        add_rows(whole, 0, ka, ra, 0, top)
-        add_rows(whole, top, kb, rb, 0, rest)
-        for k in range(REPLICAS if quarters else 0):
-            owner = (info[3] + k) % REPLICAS
-
-            @pl.loop(0, rows // PAD)
-            def _(i):
-                src = pl.ds(pl.multiple_of(owner * rows + i * PAD, PAD), PAD)
-                refs[k][pl.ds(pl.multiple_of(i * PAD, PAD), PAD), :] = whole[src, :]
-
-    ins = [info, keep_a, recv_a, keep_b, recv_b]
-    if quarters:
-        outs = [shape((rows, dim), BF)] * REPLICAS
-        scratch = [pltpu.VMEM((REPLICAS * rows, dim), BF)]
-    else:
-        outs, scratch = [shape((top + rest, dim), BF)], []
-    return vmem_call(kernel, outs, ins, "second_sum", after, scratch)
-
-
-def quarter_sum(parts, after):
-    rows, dim = parts[0].shape
-
-    def kernel(*refs):
-        out = refs[-1]
-
-        @pl.loop(0, rows // PAD)
-        def _(i):
-            at = pl.ds(pl.multiple_of(i * PAD, PAD), PAD)
-            total = refs[0][at, :].astype(F32)
-            for ref in refs[1:-1]:
-                total = total + ref[at, :].astype(F32)
-            out[at, :] = total.astype(BF)
-
-    return vmem_call(kernel, [shape((rows, dim), BF)], list(parts), "quarter_sum", after)[0]
+
+    outs = []
+    for half, rider in zip(halves, riders):
+        outs += [shape((half + rider.shape[0], dim), BF), shape((half, dim), BF)]
+    ins = [info] + [a for s in sets for a in s] + list(riders)
+    return vmem_call(kernel, outs, ins, "first_sum", after)
+
+
+def padded(rows):
+    return -(-rows // (PAD * REPLICAS)) * PAD * REPLICAS
+
+
+def split_shapes(rows, dim):
+    if lax.axis_size("replica") == REPLICAS:
+        return [shape((padded(rows) // 2, dim), BF)] * 2
+    return [shape((rows, dim), BF)]
+
+
+def sum_pieces(info, outs, pieces, rows):
+    half = padded(rows) // 2
+    if len(outs) == 1:
+        for at, one, two, start_one, start_two, count in pieces:
+            outs[0][at : at + count, :] = plus(
+                one[start_one : start_one + count, :], two[start_two : start_two + count, :]
+            )
+        return
+    for own in range(2):
+
+        @pl.when(info[3] % 2 == own)
+        def _():
+            for at, one, two, start_one, start_two, count in pieces:
+                for out, low in ((outs[1], own * half), (outs[0], (1 - own) * half)):
+                    first, last = max(at, low), min(at + count, low + half)
+                    if first < last:
+                        add_shifted(
+                            out, first - low, one, start_one + first - at, two, start_two + first - at, last - first
+                        )
+
+
+def add_shifted(out, at, one, start_one, two, start_two, count):
+    whole = count // STEP * STEP
+
+    @pl.loop(0, whole // STEP)
+    def _(i):
+        a = pl.ds(pl.multiple_of(start_one + i * STEP, PAD), STEP)
+        b = pl.ds(pl.multiple_of(start_two + i * STEP, PAD), STEP)
+        out[pl.ds(pl.multiple_of(at + i * STEP, PAD), STEP), :] = plus(one[a, :], two[b, :])
+
+    if count > whole:
+        size, done = count - whole, whole
+        out[at + done : at + count, :] = plus(
+            one[start_one + done : start_one + count, :], two[start_two + done : start_two + count, :]
+        )
+
+
+def middle_sum(info, first, along, across, third, after):
+    _, na, _, nb = first
+    dim = na.shape[1]
+    top, rest = na.shape[0], nb.shape[0]
+    half_a, half_b = (third[1].shape[0] - PAD) // 2, third[3].shape[0] // 2
+    outs = split_shapes(top + rest, dim)
+    count = len(outs)
+
+    def kernel(info, na, nb, along, across, ka, kb, *refs):
+        sums, (sa, ma, sb, mb) = refs[:count], refs[count:]
+        pieces = [(0, na, along, 0, 0, top), (top, nb, across, 0, 0, rest)]
+        sum_pieces(info, sums, pieces, top + rest)
+        for own, one, two, base, new, out, half in (
+            (info[2], ka, across, rest, ma, sa, half_a),
+            (info[1], kb, along, top, mb, sb, half_b),
+        ):
+            for part in range(2):
+                mine = own == part
+
+                @pl.when(mine)
+                def _():
+                    add_shifted(new, 0, one, part * half, two, base + part * half, half)
+
+                @pl.when(jnp.logical_not(mine))
+                def _():
+                    add_shifted(out, 0, one, part * half, two, base + part * half, half)
+
+            extra = one.shape[0] - 2 * half
+            if extra:
+                tail = plus(one[2 * half :, :], two[base + 2 * half : base + 2 * half + extra, :])
+                new[half:, :] = tail
+                out[half:, :] = tail
+
+    outs = outs + [shape((half_a + PAD, dim), BF)] * 2 + [shape((half_b, dim), BF)] * 2
+    ins = [info, na, nb, along, across, third[1], third[3]]
+    out = vmem_call(kernel, outs, ins, "middle_sum", after)
+    return out[:count], out[count:]
+
+
+def last_sum(info, kept, came, after):
+    (ka, kb), (ra, rb) = kept, came
+    dim = ka.shape[1]
+    top, rest = ka.shape[0], kb.shape[0]
+
+    def kernel(info, ka, kb, ra, rb, *outs):
+        pieces = [(0, ka, ra, 0, 0, top), (top, kb, rb, 0, 0, rest)]
+        sum_pieces(info, outs, pieces, top + rest)
+
+    outs = split_shapes(top + rest, dim)
+    return vmem_call(kernel, outs, [info, ka, kb, ra, rb], "last_sum", after)
+
+
+class Pairing:
+    def __init__(self, info, parts):
+        self.info, self.parts = info, parts
+        if self.pairs:
+            self.came = self.trade(parts[0], 1)
+        else:
+            self.parts = [lax.psum(parts[0], "replica")]
+
+    @property
+    def pairs(self):
+        return len(self.parts) == 2
+
+    def trade(self, part, bit):
+        return lax.ppermute(part, "replica", [(r, r ^ bit) for r in range(REPLICAS)])
+
+    def halve(self, after):
+        if not self.pairs:
+            return after
+        half, dim = self.parts[1].shape
+        quarter = half // 2
+
+        def kernel(info, one, two, send, keep):
+            for own in range(2):
+
+                @pl.when(info[3] // 2 == own)
+                def _():
+                    add_shifted(keep, 0, one, own * quarter, two, own * quarter, quarter)
+                    other = (1 - own) * quarter
+                    add_shifted(send, 0, one, other, two, other, quarter)
+
+        ins = [self.info, self.parts[1], self.came]
+        send, self.kept = vmem_call(kernel, [shape((quarter, dim), BF)] * 2, ins, "halve", after)
+        self.came = self.trade(send, 2)
+        return self.kept
+
+    def total(self, after):
+        if not self.pairs:
+            return after
+
+        def kernel(one, two, out):
+            add_rows(out, 0, one, two, 0, one.shape[0])
+
+        outs = [shape(self.kept.shape, BF)]
+        self.own = vmem_call(kernel, outs, [self.kept, self.came], "total", after)[0]
+        self.came = self.trade(self.own, 2)
+        return self.own
+
+    def double(self, after):
+        if not self.pairs:
+            return after
+        quarter, dim = self.own.shape
+
+        def kernel(info, one, two, out):
+            copy_rows(out, info[3] // 2 * quarter, one, 0, quarter)
+            copy_rows(out, (1 - info[3] // 2) * quarter, two, 0, quarter)
+
+        outs = [shape((2 * quarter, dim), BF)]
+        half = vmem_call(kernel, outs, [self.info, self.own, self.came], "double", after)[0]
+        self.parts = [half, self.trade(half, 1)]
+        return half
 
 
 def own_pieces(row, count, width, group):
@@ -655,8 +787,8 @@
     return pieces
 
 
-def finish(info, quarters, kind, after):
-    dim = quarters[0].shape[1]
+def finish(info, halves, kind, after):
+    dim = halves[0].shape[1]
     share = dim // GROUPS
     half = 3 * share // 2
     vectors = ((ROW_QKV, 3), (ROW_OUT, 1), (ROW_UP, 4), (ROW_DOWN, 1))
@@ -668,27 +800,26 @@
     if kind == "qkv":
         outs += [shape((1, count * dim // GROUPS), F32) for _, count in vectors]
         outs += [shape((2, share), F32)] * 2
-    rows = quarters[0].shape[0]
+    rows = halves[0].shape[0]
 
     def kernel(info, *refs):
-        given, refs = refs[: len(quarters)], refs[len(quarters) :]
+        given, refs = refs[: len(halves)], refs[len(halves) :]
         out_h = refs[:large]
         small = refs[large : len(outs)]
         src = refs[len(outs)]
         stage = refs[len(outs) + 1 : -1]
         sems = refs[-1]
-        for owner in range(len(quarters)):
-            dst, sem = src.at[pl.ds(owner * rows, rows)], sems.at[owner]
-            for k in range(len(quarters)):
-                here = (info[3] - owner + REPLICAS) % REPLICAS == k
-
-                @pl.when(here if len(quarters) > 1 else info[3] >= 0)
-                def _():
-                    pltpu.make_async_copy(given[k], dst, sem).start()
-
-        for owner in range(len(quarters)):
-            dst, sem = src.at[pl.ds(owner * rows, rows)], sems.at[owner]
-            pltpu.make_async_copy(given[0], dst, sem).wait()
+        for low in range(len(halves)):
+            here = info[3] % 2 == low if len(halves) > 1 else info[3] >= 0
+
+            @pl.when(here)
+            def _():
+                for k, part in enumerate(given):
+                    at = (low + k) % len(halves) * rows
+                    pltpu.make_async_copy(part, src.at[pl.ds(at, rows)], sems.at[k]).start()
+
+        for k, part in enumerate(given):
+            pltpu.make_async_copy(part, src.at[pl.ds(0, rows)], sems.at[k]).wait()
         if kind == "mlp":
             stage[0][...] = src[:dim, :].astype(F32)
             for i in range(4):
@@ -725,11 +856,11 @@
         for copy in copies:
             copy.wait()
 
-    scratch = [pltpu.VMEM((len(quarters) * rows, dim), BF)] + [vmem_like(o) for o in outs[:large]]
+    scratch = [pltpu.VMEM((len(halves) * rows, dim), BF)] + [vmem_like(o) for o in outs[:large]]
     places = "h" * large + "v" * (len(outs) - large)
-    ins = [info] + list(quarters)
+    ins = [info] + list(halves)
     return call(
-        kernel, outs, ins, scratch, 8, {}, "finish", after, 14, "s" + "a" * len(quarters), places
+        kernel, outs, ins, scratch, 8, {}, "finish", after, 14, "s" + "a" * len(halves), places
     )
 
 
@@ -749,24 +880,6 @@
 def exchange(a, b, turned, sections):
     ways = (ALONG, ACROSS) if turned else (ACROSS, ALONG)
     return flow(a, "group", ways[0], sections), flow(b, "group", ways[1], sections)
-
-
-def replica_send(parts):
-    if len(parts) == 1:
-        return [lax.psum(parts[0], "replica")]
-    return [shift(part, k) if k else part for k, part in enumerate(parts)]
-
-
-def shift(part, by):
-    pairs = [(i, (i + by) % REPLICAS) for i in range(REPLICAS)]
-    return lax.ppermute(part, "replica", pairs)
-
-
-def replica_sum(parts, after):
-    if len(parts) == 1:
-        return parts
-    own = quarter_sum(parts, after)
-    return [own] + [shift(own, k) for k in range(1, REPLICAS)]
 
 
 def shards(
@@ -828,23 +941,24 @@
         0, info, gmid, small, [block_input], kept_zero, params, tab_t, dx, last
     )
     third, last = qkv_grad(0, info, kept, third, last)
-    came = exchange(third[0], third[2], False, BOTH)
-
     sets = [(s[1], c[0], s[3], c[1]) for s, c in ((zero, came_zero), (one, came_one))]
-    first_mlp = first_sum(info, sets, last)
-    came_mlp = exchange(first_mlp[0], first_mlp[2], True, BOTH)
-    first_qkv = first_sum(info, [(third[1], came[0], third[3], came[1])], first_mlp[1])
-    came_qkv = exchange(first_qkv[0], first_qkv[2], True, BOTH)
-    mlp = second_sum(info, first_mlp[1], came_mlp[0], first_mlp[3], came_mlp[1], first_qkv[1])
-    last = mlp[0]
-    mlp = replica_send(mlp)
-    qkv = second_sum(info, first_qkv[1], came_qkv[0], first_qkv[3], came_qkv[1], last)
-    last = qkv[0]
-    qkv = replica_send(qkv)
-    mlp = replica_sum(mlp, last)
-    qkv = replica_sum(qkv, mlp[0])
-    grad_down, grad_up, grad_out = finish(info, mlp, "mlp", qkv[0])
-    grad_qkv, *small = finish(info, qkv, "qkv", grad_out)
+    first = first_sum(info, sets, third, last)
+    along, across = exchange(first[0], first[2], True, BOTH)
+    sums, (send_a, keep_a, send_b, keep_b) = middle_sum(
+        info, first, along, across, third, first[1]
+    )
+    mlp = Pairing(info, sums)
+    came = exchange(send_a, send_b, True, BOTH)
+    sums = last_sum(info, (keep_a, keep_b), came, keep_a)
+    qkv = Pairing(info, sums)
+    last = mlp.halve(sums[-1])
+    last = qkv.halve(last)
+    last = mlp.total(last)
+    last = qkv.total(last)
+    last = mlp.double(last)
+    last = qkv.double(last)
+    grad_down, grad_up, grad_out = finish(info, mlp.parts, "mlp", last)
+    grad_qkv, *small = finish(info, qkv.parts, "qkv", grad_out)
     qkv_b, out_b, up_b, down_b, gain, shift = small
     return (
         act[None],

time: 281 us -> 267 us (0.950)
  starting transfers between devices: 60.8 us -> 31.4 us
  waiting for transfers between devices: 128 us -> 143 us
    ppermute x12 -> x8, starting transfers between devices: 39.8 us -> 12.4 us  [trade(): lax.ppermute(part, 'replica', [(r, r ^ bit) for r in range(REPLICAS)])]
    ppermute x12 -> x8, waiting for transfers between devices: 48.7 us -> 61.9 us  [trade(): lax.ppermute(part, 'replica', [(r, r ^ bit) for r in range(REPLICAS)])]
    ppermute x6 -> x4, waiting for transfers between devices: 30.1 us -> 32.7 us  [flow(): return lax.ppermute(shard, axis, pairs)]
    ppermute x6 -> x4, starting transfers between devices: 6.11 us -> 4.07 us  [flow(): return lax.ppermute(shard, axis, pairs)]
    pallas_call x17 -> x20, Pallas kernels: 83.6 us -> 83.2 us  [call(): pl.pallas_call(body, out_shape=outs, in_specs=in_specs, out_specs=[places...]
  transfers between devices with their start and end apart: 25 -> 19, of which waited for: 11 -> 13; matrix products, arithmetic and copies ran while one was open for 0% -> 0% of each run, Pallas kernels for 13% -> 14%
where the time goes in v1:
time: 267 us; the launch traced here: 263 us
  waiting for transfers between devices  143 us (54%)
  Pallas kernels  83.2 us (31%)
  starting transfers between devices  31.4 us (12%)
  local copies, waits for them, and re-layouts  3.17 us (1%)
    pallas_call x20, Pallas kernels, call(): pl.pallas_call(body, out_shape=outs, in_specs=in_specs, out_specs=[places...  83.2 us
    ppermute x8, waiting for transfers between devices, trade(): lax.ppermute(part, 'replica', [(r, r ^ bit) for r in range(REPLICAS)])  61.9 us
    ppermute x4, waiting for transfers between devices, flow(): return lax.ppermute(shard, axis, pairs)  32.7 us
    ppermute x3, waiting for transfers between devices, to_other(): return lax.ppermute(shard, 'section', pairs)  31.7 us
    ppermute x4, waiting for transfers between devices, flow(): return lax.ppermute(shard, ('section', axis), pairs)  17.2 us
    ppermute x8, starting transfers between devices, trade(): lax.ppermute(part, 'replica', [(r, r ^ bit) for r in range(REPLICAS)])  12.4 us
    ppermute x4, starting transfers between devices, flow(): return lax.ppermute(shard, ('section', axis), pairs)  9.82 us
  transfers between devices with their start and end apart: 19, of which 13 were waited for; matrix products, arithmetic and copies ran while one was open for 0% of the time, Pallas kernels for 14%

profile of v1, /device:TPU:0, one launch (start us, length us, event | category | flops | bytes accessed | tf_op | source)
XLA Modules:
  0.0 263.3 jit_solution(11478229988551664056)
XLA Ops:
  1.5 11.7 %layer_forward.3 = (bf16[512,640]{1,0:T(8,128)(2,1)}, bf16[256,640]{1,0:T(8,128)(2,1)S(1)}, bf16[256,1920]{1,0:T(8,128)(2,1)S(1)}, bf16[20,256,256]{2,1,0:T(8,12...) custom-call(s32[4]{0:T(128)S(1)} %pad_add_fusion.info.refs_0_, ...), custom_call_target="tpu_custom_call" | custom-call | flops 115000000 | tf_op jit(solution)/shard_map/layer_forward/pallas_call | solution.py:128
  16.6 9.4 %layer_forward.4 = (bf16[512,640]{1,0:T(8,128)(2,1)}, bf16[256,640]{1,0:T(8,128)(2,1)S(1)}, bf16[256,1920]{1,0:T(8,128)(2,1)S(1)}, bf16[20,256,256]{2,1,0:T(8,12...) custom-call(s32[4]{0:T(128)S(1)} %pad_add_fusion.info.refs_0_, ...), custom_call_target="tpu_custom_call", output_to_operand_aliasing={{0}: (15, {})} | custom-call | flops 115000000 | tf_op jit(solution)/shard_map/layer_forward/pallas_call | solution.py:128
  29.6 11.6 %layer_forward.5 = (bf16[512,640]{1,0:T(8,128)(2,1)}, bf16[256,640]{1,0:T(8,128)(2,1)}, bf16[256,1920]{1,0:T(8,128)(2,1)S(1)}, bf16[20,256,256]{2,1,0:T(8,128)(2...) custom-call(s32[4]{0:T(128)S(1)} %pad_add_fusion.info.refs_0_, ...), custom_call_target="tpu_custom_call", output_to_operand_aliasing={{0}: (14, {})} | custom-call | flops 115000000 | tf_op jit(solution)/shard_map/layer_forward/pallas_call | solution.py:128
  43.7 4.4 %attention_grad.2 = (bf16[512,640]{1,0:T(8,128)(2,1)}, bf16[512,1920]{1,0:T(8,128)(2,1)S(1)}, bf16[640,512]{1,0:T(8,128)(2,1)S(1)}, f32[16,640]{1,0:T(8,128)S(1)}, f32[8,128]{1,0:T(8,128)S(1)}) custom-call(s32[4]{0:T(128)S(1)} %pad_add_fusion.info.refs_0_, f32[512,640]{1,0:T(8,128)S(1)} %get-tuple-element.108.refs_1_, bf16[640,640]{1,0:T(8,128)(2,1)S(1)} %bitcast.36, ...), custom_call_target="tpu_custom_call" | custom-call | flops 13799999488 | tf_op jit(solution)/shard_map/attention_grad/pallas_call | solution.py:128
  51.0 29.2 %collective-permute-done.2.refs_3_ = bf16[512,640]{1,0:T(8,128)(2,1)S(1)} collective-permute-done((bf16[512,640]{1,0:T(8,128)(2,1)}, bf16[512,640]{1,0:T(8,128)(2,1)S(1)}, u32[]{:S(2)}, u32[]{:S(2)}) %collective-permute-start.2) | collective-permute-done | bytes 655392 | tf_op jit(solution)/shard_map/ppermute | solution.py:921
  81.6 14.9 %mlp_grad.3 = (bf16[1280,640]{1,0:T(8,128)(2,1)}, bf16[1280,640]{1,0:T(8,128)(2,1)S(1)}, bf16[1600,640]{1,0:T(8,128)(2,1)}, bf16[1600,640]{1,0:T(8,128)(2,1)S(1)...) custom-call(s32[4]{0:T(128)S(1)} %pad_add_fusion.info.refs_0_, s32[1]{0:T(128)S(6)} %copy.42.live.refs_1_, ...), custom_call_target="tpu_custom_call" | custom-call | flops 11500000256 | tf_op jit(solution)/shard_map/mlp_grad/pallas_call | solution.py:128
  96.5 4.9 %collective-permute-start.4 = (bf16[1600,640]{1,0:T(8,128)(2,1)}, bf16[1600,640]{1,0:T(8,128)(2,1)S(1)}, u32[]{:S(2)}, u32[]{:S(2)}) collective-permute-start(bf16[1600,640]{1,0:T(8,128)(2,1)} %get-tuple-element.134), channel_id=1, source_target_pairs={{0,8},{4,12},{8,0},{12,4},{1,9},{5,13},{9,1},{13,5},{2,10},{6,14},... | collective-permute-start | bytes 6144008 | tf_op jit(solution)/shard_map/ppermute | solution.py:872
  102.2 3.4 %collective-permute-start.3 = (bf16[1280,640]{1,0:T(8,128)(2,1)}, bf16[1280,640]{1,0:T(8,128)(2,1)S(1)}, u32[]{:S(2)}, u32[]{:S(2)}) collective-permute-start(bf16[1280,640]{1,0:T(8,128)(2,1)} %get-tuple-element.132), channel_id=1, source_target_pairs={{0,4},{4,0},{8,12},{12,8},{1,5},{5,1},{9,13},{13,9},{2,6},{6,2},{1... | collective-permute-start | bytes 4915208 | tf_op jit(solution)/shard_map/ppermute | solution.py:872
  105.6 12.6 %attention_grad.3 = (bf16[512,640]{1,0:T(8,128)(2,1)}, bf16[512,1920]{1,0:T(8,128)(2,1)S(1)}, bf16[640,512]{1,0:T(8,128)(2,1)S(1)}, f32[16,640]{1,0:T(8,128)S(1)}, f32[8,128]{1,0:T(8,128)S(1)}) custom-call(s32[4]{0:T(128)S(1)} %pad_add_fusion.info.refs_0_, f32[512,640]{1,0:T(8,128)S(1)} %get-tuple-element.125.refs_1_, ...), custom_call_target="tpu_custom_call", output_to_operand_aliasing={{0}: (15, {})} | custom-call | flops 13799999488 | tf_op jit(solution)/shard_map/attention_grad/pallas_call | solution.py:128
  118.2 2.9 %qkv_grad.3 = (bf16[496,640]{1,0:T(8,128)(2,1)S(1)}, bf16[496,640]{1,0:T(8,128)(2,1)S(1)}, bf16[480,640]{1,0:T(8,128)(2,1)S(1)}, bf16[480,640]{1,0:T(8,128)(2,1)S(1)}, f32[8,128]{1,0:T(8,128)S(1)}) custom-call(s32[4]{0:T(128)S(1)} %pad_add_fusion.info.refs_0_, ...), custom_call_target="tpu_custom_call", output_to_operand_aliasing={{0}: (4, {}), {1}: (5, {}), {2}: (6, {}), {3}: (7, {})} | custom-call | flops 115000000 | tf_op jit(solution)/shard_map/qkv_grad/pallas_call | solution.py:128
  121.1 17.2 %collective-permute-done.3.refs_2_ = bf16[1280,640]{1,0:T(8,128)(2,1)S(1)} collective-permute-done((bf16[1280,640]{1,0:T(8,128)(2,1)}, bf16[1280,640]{1,0:T(8,128)(2,1)S(1)}, u32[]{:S(2)}, u32[]{:S(2)}) %collective-permute-start.3) | collective-permute-done | bytes 1638432 | tf_op jit(solution)/shard_map/ppermute | solution.py:872
  142.2 20.3 %collective-permute-done.7.refs_3_ = bf16[1120,640]{1,0:T(8,128)(2,1)S(1)} collective-permute-done((bf16[1120,640]{1,0:T(8,128)(2,1)S(1)}, bf16[1120,640]{1,0:T(8,128)(2,1)S(1)}, u32[]{:S(2)}, u32[]{:S(2)}) %collective-permute-start.7) | collective-permute-done | bytes 1433632 | tf_op jit(solution)/shard_map/ppermute | solution.py:869
  162.5 7.1 %collective-permute-done.8.refs_4_ = bf16[1296,640]{1,0:T(8,128)(2,1)S(1)} collective-permute-done((bf16[1296,640]{1,0:T(8,128)(2,1)S(1)}, bf16[1296,640]{1,0:T(8,128)(2,1)S(1)}, u32[]{:S(2)}, u32[]{:S(2)}) %collective-permute-start.8) | collective-permute-done | bytes 1658912 | tf_op jit(solution)/shard_map/ppermute | solution.py:869
  174.7 5.4 %collective-permute-done.10.refs_4_ = bf16[240,640]{1,0:T(8,128)(2,1)S(1)} collective-permute-done((bf16[240,640]{1,0:T(8,128)(2,1)S(1)}, bf16[240,640]{1,0:T(8,128)(2,1)S(1)}, u32[]{:S(2)}, u32[]{:S(2)}) %collective-permute-start.10) | collective-permute-done | bytes 307232 | tf_op jit(solution)/shard_map/ppermute | solution.py:869
  180.9 12.1 %collective-permute-done.12.refs_2_ = bf16[736,640]{1,0:T(8,128)(2,1)S(1)} collective-permute-done((bf16[736,640]{1,0:T(8,128)(2,1)S(1)}, bf16[736,640]{1,0:T(8,128)(2,1)S(1)}, u32[]{:S(2)}, u32[]{:S(2)}) %collective-permute-start.12) | collective-permute-done | bytes 942112 | tf_op jit(solution)/shard_map/ppermute | solution.py:731
  195.9 9.4 %collective-permute-done.11.refs_2_ = bf16[256,640]{1,0:T(8,128)(2,1)S(1)} collective-permute-done((bf16[256,640]{1,0:T(8,128)(2,1)S(1)}, bf16[256,640]{1,0:T(8,128)(2,1)S(1)}, u32[]{:S(2)}, u32[]{:S(2)}) %collective-permute-start.11) | collective-permute-done | bytes 327712 | tf_op jit(solution)/shard_map/ppermute | solution.py:731
  206.0 8.0 %collective-permute-done.14.refs_1_ = bf16[368,640]{1,0:T(8,128)(2,1)S(1)} collective-permute-done((bf16[368,640]{1,0:T(8,128)(2,1)S(1)}, bf16[368,640]{1,0:T(8,128)(2,1)S(1)}, u32[]{:S(2)}, u32[]{:S(2)}) %collective-permute-start.14) | collective-permute-done | bytes 471072 | tf_op jit(solution)/shard_map/ppermute | solution.py:731
  214.3 2.9 %collective-permute-start.13 = (bf16[128,640]{1,0:T(8,128)(2,1)S(1)}, bf16[128,640]{1,0:T(8,128)(2,1)S(1)}, u32[]{:S(2)}, u32[]{:S(2)}) collective-permute-start(bf16[128,640]{1,0:T(8,128)(2,1)S(1)} %get-tuple-element.166), channel_id=1, source_target_pairs={{0,2},{1,3},{2,0},{3,1},{4,6},{5,7},{6,4},{7,5},{8,10},{9,11},{10,... | collective-permute-start | bytes 491528 | tf_op jit(solution)/shard_map/ppermute | solution.py:731
  217.2 16.4 %collective-permute-done.13.refs_1_ = bf16[128,640]{1,0:T(8,128)(2,1)S(1)} collective-permute-done((bf16[128,640]{1,0:T(8,128)(2,1)S(1)}, bf16[128,640]{1,0:T(8,128)(2,1)S(1)}, u32[]{:S(2)}, u32[]{:S(2)}) %collective-permute-start.13) | collective-permute-done | bytes 163872 | tf_op jit(solution)/shard_map/ppermute | solution.py:731
  234.4 2.5 collective-permute-start.15
  236.9 13.9 %collective-permute-done.15.refs_2_ = bf16[128,640]{1,0:T(8,128)(2,1)S(1)} collective-permute-done((bf16[128,640]{1,0:T(8,128)(2,1)S(1)}, bf16[128,640]{1,0:T(8,128)(2,1)S(1)}, u32[]{:S(2)}, u32[]{:S(2)}) %collective-permute-start.15) | collective-permute-done | bytes 163872 | tf_op jit(solution)/shard_map/ppermute | solution.py:731
  251.4 3.1 %collective-permute-start.17 = (bf16[256,640]{1,0:T(8,128)(2,1)S(1)}, bf16[256,640]{1,0:T(8,128)(2,1)S(1)}, u32[]{:S(2)}, u32[]{:S(2)}) collective-permute-start(bf16[256,640]{1,0:T(8,128)(2,1)S(1)} %double.3.refs_3_.refs_1_), channel_id=1, source_target_pairs={{0,1},{1,0},{2,3},{3,2},{4,5},{5,4},{6,7},{7,6},{8,9},{9,8},{10,11... | collective-permute-start | bytes 983048 | tf_op jit(solution)/shard_map/ppermute | solution.py:731
  254.5 3.1 %finish.2 = (f32[640,640]{1,0:T(8,128)}, f32[160,2560]{1,0:T(8,128)}, f32[160,640]{1,0:T(8,128)}) custom-call(s32[4]{0:T(128)S(1)} %pad_add_fusion.info.refs_0_, bf16[736,640]{1,0:T(8,128)(2,1)S(1)} %double.2.refs_3_.refs_1_, bf16[736,640]{1,0:T(8,128)(2,1)S(1)} %collective-permute-done.18.refs_2_, bf16[256,640]{1,0:T(8,128)(2,1)S(1)} %double.3.refs_3_.refs_1_), custom_call_target="tpu_custom_call" | custom-call | flops 115000000 | tf_op jit(solution)/shard_map/finish/pallas_call | solution.py:128
  260.5 2.5 finish.3
  (91 shorter events, 32.3 us)
Async XLA Ops:
  14.0 2.5 collective-permute-start
  26.1 3.5 %collective-permute-start.1 = (bf16[256,640]{1,0:T(8,128)(2,1)S(1)}, bf16[256,640]{1,0:T(8,128)(2,1)S(1)}, u32[]{:S(2)}, u32[]{:S(2)}) collective-permute-start(bf16[256,640]{1,0:T(8,128)(2,1)S(1)} %get-tuple-element.97), channel_id=1, source_target_pairs={{0,16},{1,17},{2,18},{3,19},{4,20},{5,21},{6,22},{7,23},{8,24},{9,... | collective-permute-start | bytes 983048 | tf_op jit(solution)/shard_map/ppermute | solution.py:921
  43.7 36.5 %copy-start.23 = (f32[256,640]{1,0:T(8,128)S(1)}, f32[256,640]{1,0:T(8,128)}, u32[]{:S(2)}) copy-start(f32[256,640]{1,0:T(8,128)} %copy-done.22) | copy-start | bytes 1966084
  43.7 36.5 %copy-start.25 = (bf16[640,256]{1,0:T(8,128)(2,1)S(1)}, bf16[640,256]{1,0:T(8,128)(2,1)}, u32[]{:S(2)}) copy-start(bf16[640,256]{1,0:T(8,128)(2,1)} %copy-done.24) | copy-start | bytes 983044
  48.1 32.1 %copy-start.14 = (bf16[256,2560]{1,0:T(8,128)(2,1)S(1)}, bf16[256,2560]{1,0:T(8,128)(2,1)}, u32[]{:S(2)}) copy-start(bf16[256,2560]{1,0:T(8,128)(2,1)} %copy-done.13) | copy-start | bytes 3932164
  48.1 32.1 %copy-start.16 = (bf16[256,2560]{1,0:T(8,128)(2,1)S(1)}, bf16[256,2560]{1,0:T(8,128)(2,1)}, u32[]{:S(2)}) copy-start(bf16[256,2560]{1,0:T(8,128)(2,1)} %copy-done.15) | copy-start | bytes 3932164
  48.1 32.1 %collective-permute-start.2 = (bf16[512,640]{1,0:T(8,128)(2,1)}, bf16[512,640]{1,0:T(8,128)(2,1)S(1)}, u32[]{:S(2)}, u32[]{:S(2)}) collective-permute-start(bf16[512,640]{1,0:T(8,128)(2,1)} %get-tuple-element.115.refs_15_), channel_id=1, source_target_pairs={{16,0},{17,1},{18,2},{19,3},{20,4},{21,5},{22,6},{23,7},{24,8},{25... | collective-permute-start | bytes 1966088 | tf_op jit(solution)/shard_map/ppermute | solution.py:921
  49.7 71.4 %collective-permute-start.6 = (bf16[1600,640]{1,0:T(8,128)(2,1)}, bf16[1600,640]{1,0:T(8,128)(2,1)S(1)}, u32[]{:S(2)}, u32[]{:S(2)}) collective-permute-start(bf16[1600,640]{1,0:T(8,128)(2,1)} %get-tuple-element.138), channel_id=1, source_target_pairs={{16,24},{20,28},{24,16},{28,20},{17,25},{21,29},{25,17},{29,21},{1... | collective-permute-start | bytes 6144008 | tf_op jit(solution)/shard_map/ppermute | solution.py:872
  81.6 24.0 %copy-start.20 = (bf16[256,1920]{1,0:T(8,128)(2,1)S(1)}, bf16[256,1920]{1,0:T(8,128)(2,1)}, u32[]{:S(2)}) copy-start(bf16[256,1920]{1,0:T(8,128)(2,1)} %copy-done.19) | copy-start | bytes 2949124
  96.5 41.8 %collective-permute-start.4 = (bf16[1600,640]{1,0:T(8,128)(2,1)}, bf16[1600,640]{1,0:T(8,128)(2,1)S(1)}, u32[]{:S(2)}, u32[]{:S(2)}) collective-permute-start(bf16[1600,640]{1,0:T(8,128)(2,1)} %get-tuple-element.134), channel_id=1, source_target_pairs={{0,8},{4,12},{8,0},{12,4},{1,9},{5,13},{9,1},{13,5},{2,10},{6,14},... | collective-permute-start | bytes 6144008 | tf_op jit(solution)/shard_map/ppermute | solution.py:872
  101.4 19.7 %collective-permute-start.5 = (bf16[1280,640]{1,0:T(8,128)(2,1)}, bf16[1280,640]{1,0:T(8,128)(2,1)S(1)}, u32[]{:S(2)}, u32[]{:S(2)}) collective-permute-start(bf16[1280,640]{1,0:T(8,128)(2,1)} %get-tuple-element.136), channel_id=1, source_target_pairs={{16,20},{20,16},{24,28},{28,24},{17,21},{21,17},{25,29},{29,25},{1... | collective-permute-start | bytes 4915208 | tf_op jit(solution)/shard_map/ppermute | solution.py:872
  102.2 36.2 %collective-permute-start.3 = (bf16[1280,640]{1,0:T(8,128)(2,1)}, bf16[1280,640]{1,0:T(8,128)(2,1)S(1)}, u32[]{:S(2)}, u32[]{:S(2)}) collective-permute-start(bf16[1280,640]{1,0:T(8,128)(2,1)} %get-tuple-element.132), channel_id=1, source_target_pairs={{0,4},{4,0},{8,12},{12,8},{1,5},{5,1},{9,13},{13,9},{2,6},{6,2},{1... | collective-permute-start | bytes 4915208 | tf_op jit(solution)/shard_map/ppermute | solution.py:872
  140.2 29.4 %collective-permute-start.8 = (bf16[1296,640]{1,0:T(8,128)(2,1)S(1)}, bf16[1296,640]{1,0:T(8,128)(2,1)S(1)}, u32[]{:S(2)}, u32[]{:S(2)}) collective-permute-start(bf16[1296,640]{1,0:T(8,128)(2,1)S(1)} %get-tuple-element.153), channel_id=1, source_target_pairs={{0,4},{4,0},{8,12},{12,8},{1,5},{5,1},{9,13},{13,9},{2,6},{6,2},{1... | collective-permute-start | bytes 4976648 | tf_op jit(solution)/shard_map/ppermute | solution.py:869
  141.7 20.8 %collective-permute-start.7 = (bf16[1120,640]{1,0:T(8,128)(2,1)S(1)}, bf16[1120,640]{1,0:T(8,128)(2,1)S(1)}, u32[]{:S(2)}, u32[]{:S(2)}) collective-permute-start(bf16[1120,640]{1,0:T(8,128)(2,1)S(1)} %get-tuple-element.152), channel_id=1, source_target_pairs={{0,8},{4,12},{8,0},{12,4},{1,9},{5,13},{9,1},{13,5},{2,10},{6,14},... | collective-permute-start | bytes 4300808 | tf_op jit(solution)/shard_map/ppermute | solution.py:869
  171.1 21.9 %collective-permute-start.12 = (bf16[736,640]{1,0:T(8,128)(2,1)S(1)}, bf16[736,640]{1,0:T(8,128)(2,1)S(1)}, u32[]{:S(2)}, u32[]{:S(2)}) collective-permute-start(bf16[736,640]{1,0:T(8,128)(2,1)S(1)} %get-tuple-element.163), channel_id=1, source_target_pairs={{0,1},{1,0},{2,3},{3,2},{4,5},{5,4},{6,7},{7,6},{8,9},{9,8},{10,11... | collective-permute-start | bytes 2826248 | tf_op jit(solution)/shard_map/ppermute | solution.py:731
  172.7 7.4 %collective-permute-start.9 = (bf16[256,640]{1,0:T(8,128)(2,1)S(1)}, bf16[256,640]{1,0:T(8,128)(2,1)S(1)}, u32[]{:S(2)}, u32[]{:S(2)}) collective-permute-start(bf16[256,640]{1,0:T(8,128)(2,1)S(1)} %get-tuple-element.158), channel_id=1, source_target_pairs={{0,8},{4,12},{8,0},{12,4},{1,9},{5,13},{9,1},{13,5},{2,10},{6,14},... | collective-permute-start | bytes 983048 | tf_op jit(solution)/shard_map/ppermute | solution.py:869
  173.2 6.9 %collective-permute-start.10 = (bf16[240,640]{1,0:T(8,128)(2,1)S(1)}, bf16[240,640]{1,0:T(8,128)(2,1)S(1)}, u32[]{:S(2)}, u32[]{:S(2)}) collective-permute-start(bf16[240,640]{1,0:T(8,128)(2,1)S(1)} %get-tuple-element.159), channel_id=1, source_target_pairs={{0,4},{4,0},{8,12},{12,8},{1,5},{5,1},{9,13},{13,9},{2,6},{6,2},{1... | collective-permute-start | bytes 921608 | tf_op jit(solution)/shard_map/ppermute | solution.py:869
  193.8 20.2 %collective-permute-start.14 = (bf16[368,640]{1,0:T(8,128)(2,1)S(1)}, bf16[368,640]{1,0:T(8,128)(2,1)S(1)}, u32[]{:S(2)}, u32[]{:S(2)}) collective-permute-start(bf16[368,640]{1,0:T(8,128)(2,1)S(1)} %get-tuple-element.167), channel_id=1, source_target_pairs={{0,2},{1,3},{2,0},{3,1},{4,6},{5,7},{6,4},{7,5},{8,10},{9,11},{10,... | collective-permute-start | bytes 1413128 | tf_op jit(solution)/shard_map/ppermute | solution.py:731
  193.9 11.5 %collective-permute-start.11 = (bf16[256,640]{1,0:T(8,128)(2,1)S(1)}, bf16[256,640]{1,0:T(8,128)(2,1)S(1)}, u32[]{:S(2)}, u32[]{:S(2)}) collective-permute-start(bf16[256,640]{1,0:T(8,128)(2,1)S(1)} %get-tuple-element.161), channel_id=1, source_target_pairs={{0,1},{1,0},{2,3},{3,2},{4,5},{5,4},{6,7},{7,6},{8,9},{9,8},{10,11... | collective-permute-start | bytes 983048 | tf_op jit(solution)/shard_map/ppermute | solution.py:731
  214.2 19.4 %collective-permute-start.16 = (bf16[368,640]{1,0:T(8,128)(2,1)S(1)}, bf16[368,640]{1,0:T(8,128)(2,1)S(1)}, u32[]{:S(2)}, u32[]{:S(2)}) collective-permute-start(bf16[368,640]{1,0:T(8,128)(2,1)S(1)} %total.2.refs_2_.refs_1_), channel_id=1, source_target_pairs={{0,2},{1,3},{2,0},{3,1},{4,6},{5,7},{6,4},{7,5},{8,10},{9,11},{10,... | collective-permute-start | bytes 1413128 | tf_op jit(solution)/shard_map/ppermute | solution.py:731
  214.3 19.3 %collective-permute-start.13 = (bf16[128,640]{1,0:T(8,128)(2,1)S(1)}, bf16[128,640]{1,0:T(8,128)(2,1)S(1)}, u32[]{:S(2)}, u32[]{:S(2)}) collective-permute-start(bf16[128,640]{1,0:T(8,128)(2,1)S(1)} %get-tuple-element.166), channel_id=1, source_target_pairs={{0,2},{1,3},{2,0},{3,1},{4,6},{5,7},{6,4},{7,5},{8,10},{9,11},{10,... | collective-permute-start | bytes 491528 | tf_op jit(solution)/shard_map/ppermute | solution.py:731
  234.3 20.2 %collective-permute-start.18 = (bf16[736,640]{1,0:T(8,128)(2,1)S(1)}, bf16[736,640]{1,0:T(8,128)(2,1)S(1)}, u32[]{:S(2)}, u32[]{:S(2)}) collective-permute-start(bf16[736,640]{1,0:T(8,128)(2,1)S(1)} %double.2.refs_3_.refs_1_), channel_id=1, source_target_pairs={{0,1},{1,0},{2,3},{3,2},{4,5},{5,4},{6,7},{7,6},{8,9},{9,8},{10,11... | collective-permute-start | bytes 2826248 | tf_op jit(solution)/shard_map/ppermute | solution.py:731
  234.4 16.4 %collective-permute-start.15 = (bf16[128,640]{1,0:T(8,128)(2,1)S(1)}, bf16[128,640]{1,0:T(8,128)(2,1)S(1)}, u32[]{:S(2)}, u32[]{:S(2)}) collective-permute-start(bf16[128,640]{1,0:T(8,128)(2,1)S(1)} %total.3.refs_3_.refs_1_), channel_id=1, source_target_pairs={{0,2},{1,3},{2,0},{3,1},{4,6},{5,7},{6,4},{7,5},{8,10},{9,11},{10,... | collective-permute-start | bytes 491528 | tf_op jit(solution)/shard_map/ppermute | solution.py:731
  251.4 8.1 %collective-permute-start.17 = (bf16[256,640]{1,0:T(8,128)(2,1)S(1)}, bf16[256,640]{1,0:T(8,128)(2,1)S(1)}, u32[]{:S(2)}, u32[]{:S(2)}) collective-permute-start(bf16[256,640]{1,0:T(8,128)(2,1)S(1)} %double.3.refs_3_.refs_1_), channel_id=1, source_target_pairs={{0,1},{1,0},{2,3},{3,2},{4,5},{5,4},{6,7},{7,6},{8,9},{9,8},{10,11... | collective-permute-start | bytes 983048 | tf_op jit(solution)/shard_map/ppermute | solution.py:731
  (23 other events, 276.6 us)

commit v2 on v1

--- a/solution.py
+++ b/solution.py
@@ -587,32 +587,29 @@
         out[pl.ds(pl.multiple_of(at + whole, PAD), count - whole), :] = src[lines, :]
 
 
-def first_sum(info, sets, third, after):
+def first_sum(section, info, held, came, third, after):
     dim = third[0].shape[1]
-    halves = [k.shape[0] // 2 for k in sets[0][::2]]
+    halves = [k.shape[0] // 2 for k in (held[1], held[3])]
     riders = (third[2], third[0])
 
-    def kernel(info, *refs):
-        given = refs[4 * len(sets) : 4 * len(sets) + 2]
-        sa, na, sb, nb = refs[4 * len(sets) + 2 :]
-        for out, half, rider in ((sa, halves[0], given[0]), (sb, halves[1], given[1])):
-            copy_rows(out, half, rider, 0, rider.shape[0])
-        for section in range(len(sets)):
-            ka, ra, kb, rb = refs[4 * section : 4 * section + 4]
-
-            @pl.when(info[0] == section)
-            def _():
-                for own, one, two, new, out, half in (
-                    (info[2], ka, ra, na, sa, halves[0]),
-                    (info[1], kb, rb, nb, sb, halves[1]),
-                ):
-                    add_rows(out, 0, one, two, (1 - own) * half, half)
-                    add_rows(new, 0, one, two, own * half, half)
+    def kernel(info, ka, ra, kb, rb, *refs):
+        given = refs[:2]
+        sa, na, sb, nb = refs[2:]
+
+        @pl.when(info[0] == section)
+        def _():
+            for own, one, two, new, out, half, rider in (
+                (info[2], ka, ra, na, sa, halves[0], given[0]),
+                (info[1], kb, rb, nb, sb, halves[1], given[1]),
+            ):
+                add_rows(out, 0, one, two, (1 - own) * half, half)
+                add_rows(new, 0, one, two, own * half, half)
+                copy_rows(out, half, rider, 0, rider.shape[0])
 
     outs = []
     for half, rider in zip(halves, riders):
         outs += [shape((half + rider.shape[0], dim), BF), shape((half, dim), BF)]
-    ins = [info] + [a for s in sets for a in s] + list(riders)
+    ins = [info, held[1], came[0], held[3], came[1]] + list(riders)
     return vmem_call(kernel, outs, ins, "first_sum", after)
 
 
@@ -657,62 +654,63 @@
         out[pl.ds(pl.multiple_of(at + i * STEP, PAD), STEP), :] = plus(one[a, :], two[b, :])
 
     if count > whole:
-        size, done = count - whole, whole
-        out[at + done : at + count, :] = plus(
-            one[start_one + done : start_one + count, :], two[start_two + done : start_two + count, :]
-        )
-
-
-def middle_sum(info, first, along, across, third, after):
-    _, na, _, nb = first
-    dim = na.shape[1]
-    top, rest = na.shape[0], nb.shape[0]
+        a = pl.ds(pl.multiple_of(start_one + whole, PAD), count - whole)
+        b = pl.ds(pl.multiple_of(start_two + whole, PAD), count - whole)
+        out[pl.ds(pl.multiple_of(at + whole, PAD), count - whole), :] = plus(one[a, :], two[b, :])
+
+
+def third_sum(info, flows, third, after):
+    dim = third[1].shape[1]
     half_a, half_b = (third[1].shape[0] - PAD) // 2, third[3].shape[0] // 2
-    outs = split_shapes(top + rest, dim)
-    count = len(outs)
-
-    def kernel(info, na, nb, along, across, ka, kb, *refs):
-        sums, (sa, ma, sb, mb) = refs[:count], refs[count:]
-        pieces = [(0, na, along, 0, 0, top), (top, nb, across, 0, 0, rest)]
-        sum_pieces(info, sums, pieces, top + rest)
-        for own, one, two, base, new, out, half in (
-            (info[2], ka, across, rest, ma, sa, half_a),
-            (info[1], kb, along, top, mb, sb, half_b),
-        ):
-            for part in range(2):
-                mine = own == part
-
-                @pl.when(mine)
-                def _():
-                    add_shifted(new, 0, one, part * half, two, base + part * half, half)
-
-                @pl.when(jnp.logical_not(mine))
-                def _():
-                    add_shifted(out, 0, one, part * half, two, base + part * half, half)
-
-            extra = one.shape[0] - 2 * half
-            if extra:
-                tail = plus(one[2 * half :, :], two[base + 2 * half : base + 2 * half + extra, :])
-                new[half:, :] = tail
-                out[half:, :] = tail
-
-    outs = outs + [shape((half_a + PAD, dim), BF)] * 2 + [shape((half_b, dim), BF)] * 2
-    ins = [info, na, nb, along, across, third[1], third[3]]
-    out = vmem_call(kernel, outs, ins, "middle_sum", after)
-    return out[:count], out[count:]
-
-
-def last_sum(info, kept, came, after):
-    (ka, kb), (ra, rb) = kept, came
-    dim = ka.shape[1]
-    top, rest = ka.shape[0], kb.shape[0]
-
-    def kernel(info, ka, kb, ra, rb, *outs):
-        pieces = [(0, ka, ra, 0, 0, top), (top, kb, rb, 0, 0, rest)]
-        sum_pieces(info, outs, pieces, top + rest)
-
-    outs = split_shapes(top + rest, dim)
-    return vmem_call(kernel, outs, [info, ka, kb, ra, rb], "last_sum", after)
+    top, rest = flows[0][0].shape[0] - 2 * half_b, flows[0][1].shape[0] - 2 * half_a - PAD
+
+    def kernel(info, ka, kb, *refs):
+        sa, ma, sb, mb = refs[4:]
+        for section in range(2):
+            along, across = refs[2 * section : 2 * section + 2]
+
+            @pl.when(info[0] == section)
+            def _():
+                for own, one, two, base, new, out, half in (
+                    (info[2], ka, across, rest, ma, sa, half_a),
+                    (info[1], kb, along, top, mb, sb, half_b),
+                ):
+                    for target, part in ((new, own), (out, 1 - own)):
+                        add_shifted(target, 0, one, part * half, two, base + part * half, half)
+                    extra = one.shape[0] - 2 * half
+                    if extra:
+                        low = base + 2 * half
+                        tail = plus(one[2 * half :, :], two[low : low + extra, :])
+                        new[half:, :] = tail
+                        out[half:, :] = tail
+
+    outs = [shape((half_a + PAD, dim), BF)] * 2 + [shape((half_b, dim), BF)] * 2
+    ins = [info, third[1], third[3]] + [a for f in flows for a in f]
+    return vmem_call(kernel, outs, ins, "third_sum", after)
+
+
+def last_sum(info, kept, flows, kept_third, came_third, after):
+    dim = kept[0][0].shape[1]
+    rows = [a.shape[0] for a in kept[0]] + [a.shape[0] for a in kept_third]
+    starts = [sum(rows[:i]) for i in range(4)]
+
+    def kernel(info, *refs):
+        ka, kb, ra, rb = refs[8:12]
+        outs = refs[12:]
+        for section in range(2):
+            na, nb, along, across = refs[4 * section : 4 * section + 4]
+
+            @pl.when(info[0] == section)
+            def _():
+                pairs = ((na, along), (nb, across), (ka, ra), (kb, rb))
+                pieces = [(at, a, b, 0, 0, n) for at, (a, b), n in zip(starts, pairs, rows)]
+                sum_pieces(info, outs, pieces, sum(rows))
+
+    outs = split_shapes(sum(rows), dim)
+    ins = [info]
+    for k, f in zip(kept, flows):
+        ins += list(k) + list(f)
+    return vmem_call(kernel, outs, ins + list(kept_third) + list(came_third), "last_sum", after)
 
 
 class Pairing:
@@ -787,19 +785,21 @@
     return pieces
 
 
-def finish(info, halves, kind, after):
+def finish(info, halves, after):
     dim = halves[0].shape[1]
     share = dim // GROUPS
     half = 3 * share // 2
+    base = dim + 5 * share
     vectors = ((ROW_QKV, 3), (ROW_OUT, 1), (ROW_UP, 4), (ROW_DOWN, 1))
-    if kind == "mlp":
-        outs = [shape((dim, dim), F32), shape((share, 4 * dim), F32), shape((share, dim), F32)]
-    else:
-        outs = [shape((share, 3 * dim), F32)]
+    outs = [
+        shape((dim, dim), F32),
+        shape((share, 4 * dim), F32),
+        shape((share, dim), F32),
+        shape((share, 3 * dim), F32),
+    ]
     large = len(outs)
-    if kind == "qkv":
-        outs += [shape((1, count * dim // GROUPS), F32) for _, count in vectors]
-        outs += [shape((2, share), F32)] * 2
+    outs += [shape((1, count * dim // GROUPS), F32) for _, count in vectors]
+    outs += [shape((2, share), F32)] * 2
     rows = halves[0].shape[0]
 
     def kernel(info, *refs):
@@ -820,38 +820,40 @@
 
         for k, part in enumerate(given):
             pltpu.make_async_copy(part, src.at[pl.ds(0, rows)], sems.at[k]).wait()
-        if kind == "mlp":
-            stage[0][...] = src[:dim, :].astype(F32)
-            for i in range(4):
-                block = src[dim + i * share : dim + (i + 1) * share, :].astype(F32)
-                stage[1][:, i * dim : (i + 1) * dim] = block
-            stage[2][...] = src[dim + 4 * share : dim + 5 * share, :].astype(F32)
-        else:
-            for i in range(3):
-                at, left, to = i * share, share, 0
-                while left:
-                    count = min(left, half - at % half)
-                    row = at if at < half else at + PAD
-                    block = src[row : row + count, :].astype(F32)
-                    stage[0][to : to + count, i * dim : (i + 1) * dim] = block
-                    at, left, to = at + count, left - count, to + count
-        copies = [
-            pltpu.make_async_copy(s, o, sems.at[REPLICAS + i])
-            for i, (s, o) in enumerate(zip(stage, out_h))
-        ]
-        for copy in copies:
+        copies = []
+
+        def save(i):
+            copy = pltpu.make_async_copy(stage[i], out_h[i], sems.at[2 + i])
             copy.start()
-        if kind == "qkv":
-            tail = src[half : half + PAD, :].astype(F32)
-            for group in range(GROUPS):
-
-                @pl.when(info[1] + 2 * info[2] == group)
-                def _():
-                    for out, (row, count) in zip(small, vectors):
-                        for r, c, size, at in own_pieces(row, count, dim, group):
-                            out[:, at : at + size] = tail[r : r + 1, c : c + size]
-                    for out, row in zip(small[4:], (ROW_GAIN, ROW_SHIFT)):
-                        out[...] = tail[row : row + 2, group * share : (group + 1) * share]
+            copies.append(copy)
+
+        stage[0][...] = src[:dim, :].astype(F32)
+        save(0)
+        for i in range(4):
+            block = src[dim + i * share : dim + (i + 1) * share, :].astype(F32)
+            stage[1][:, i * dim : (i + 1) * dim] = block
+        save(1)
+        for i in range(3):
+            at, left, to = i * share, share, 0
+            while left:
+                count = min(left, half - at % half)
+                row = base + (at if at < half else at + PAD)
+                block = src[row : row + count, :].astype(F32)
+                stage[3][to : to + count, i * dim : (i + 1) * dim] = block
+                at, left, to = at + count, left - count, to + count
+        save(3)
+        stage[2][...] = src[dim + 4 * share : base, :].astype(F32)
+        save(2)
+        tail = src[base + half : base + half + PAD, :].astype(F32)
+        for group in range(GROUPS):
+
+            @pl.when(info[1] + 2 * info[2] == group)
+            def _():
+                for out, (row, count) in zip(small, vectors):
+                    for r, c, size, at in own_pieces(row, count, dim, group):
+                        out[:, at : at + size] = tail[r : r + 1, c : c + size]
+                for out, row in zip(small[4:], (ROW_GAIN, ROW_SHIFT)):
+                    out[...] = tail[row : row + 2, group * share : (group + 1) * share]
 
         for copy in copies:
             copy.wait()
@@ -860,7 +862,7 @@
     places = "h" * large + "v" * (len(outs) - large)
     ins = [info] + list(halves)
     return call(
-        kernel, outs, ins, scratch, 8, {}, "finish", after, 14, "s" + "a" * len(halves), places
+        kernel, outs, ins, scratch, 8, {}, "finish", after, 16, "s" + "a" * len(halves), places
     )
 
 
@@ -929,36 +931,31 @@
 
     common = (info, crop_count, mask_count)
     one, gmid, small, last = mlp_grad(1, *common, cotangent, kept_one, params, None)
-    came_one = exchange(one[0], one[2], False, (1,))
+    came = exchange(one[0], one[2], False, (1,))
     dx, kept, last = attention_grad(
         1, info, gmid, small, arrived, kept_one, params, tab_t, None, last
     )
     grad_back = to_other(dx, [(1, 0)])
     third, last = qkv_grad(1, info, kept, None, last)
-    zero, gmid, small, last = mlp_grad(0, *common, grad_back, kept_zero, params, last)
-    came_zero = exchange(zero[0], zero[2], False, (0,))
+    one = first_sum(1, info, one, came, third, last)
+    came_one = exchange(one[0], one[2], True, (1,))
+    zero, gmid, small, last = mlp_grad(0, *common, grad_back, kept_zero, params, one[1])
+    came = exchange(zero[0], zero[2], False, (0,))
     dx, kept, last = attention_grad(
         0, info, gmid, small, [block_input], kept_zero, params, tab_t, dx, last
     )
     third, last = qkv_grad(0, info, kept, third, last)
-    sets = [(s[1], c[0], s[3], c[1]) for s, c in ((zero, came_zero), (one, came_one))]
-    first = first_sum(info, sets, third, last)
-    along, across = exchange(first[0], first[2], True, BOTH)
-    sums, (send_a, keep_a, send_b, keep_b) = middle_sum(
-        info, first, along, across, third, first[1]
-    )
-    mlp = Pairing(info, sums)
+    zero = first_sum(0, info, zero, came, third, last)
+    came_zero = exchange(zero[0], zero[2], True, (0,))
+    flows = (came_zero, came_one)
+    send_a, keep_a, send_b, keep_b = third_sum(info, flows, third, zero[1])
     came = exchange(send_a, send_b, True, BOTH)
-    sums = last_sum(info, (keep_a, keep_b), came, keep_a)
-    qkv = Pairing(info, sums)
-    last = mlp.halve(sums[-1])
-    last = qkv.halve(last)
-    last = mlp.total(last)
-    last = qkv.total(last)
-    last = mlp.double(last)
-    last = qkv.double(last)
-    grad_down, grad_up, grad_out = finish(info, mlp.parts, "mlp", last)
-    grad_qkv, *small = finish(info, qkv.parts, "qkv", grad_out)
+    kept = ((zero[1], zero[3]), (one[1], one[3]))
+    total = Pairing(info, last_sum(info, kept, flows, (keep_a, keep_b), came, keep_a))
+    last = total.halve(None)
+    last = total.total(None)
+    last = total.double(None)
+    grad_down, grad_up, grad_out, grad_qkv, *small = finish(info, total.parts, None)
     qkv_b, out_b, up_b, down_b, gain, shift = small
     return (
         act[None],

time: 267 us -> 269 us (level)
  waiting for transfers between devices: 143 us -> 156 us
  starting transfers between devices: 31.4 us -> 26.7 us
  Pallas kernels: 83.2 us -> 79.5 us
    ppermute x4 -> x2, waiting for transfers between devices: 32.7 us -> 6.33 us  [flow(): return lax.ppermute(shard, axis, pairs)]
    ppermute x4 -> x8, waiting for transfers between devices: 17.2 us -> 40.1 us  [flow(): return lax.ppermute(shard, ('section', axis), pairs)]
    ppermute x8 -> x4, waiting for transfers between devices: 61.9 us -> 73.6 us  [trade(): lax.ppermute(part, 'replica', [(r, r ^ bit) for r in range(REPLICAS)])]
    ppermute x8 -> x4, starting transfers between devices: 12.4 us -> 8.17 us  [trade(): lax.ppermute(part, 'replica', [(r, r ^ bit) for r in range(REPLICAS)])]
    ppermute x3, waiting for transfers between devices: 31.7 us -> 35.5 us  [to_other(): return lax.ppermute(shard, 'section', pairs)]
    pallas_call x20 -> x17, Pallas kernels: 83.2 us -> 79.5 us  [call(): pl.pallas_call(body, out_shape=outs, in_specs=in_specs, out_specs=[places...]
    ppermute x4 -> x8, starting transfers between devices: 9.82 us -> 11.6 us  [flow(): return lax.ppermute(shard, ('section', axis), pairs)]
  transfers between devices with their start and end apart: 19 -> 17, of which waited for: 13 -> 12; matrix products, arithmetic and copies ran while one was open for 0% -> 0% of each run, Pallas kernels for 14% -> 9%
where the time goes in v2:
time: 269 us; the launch traced here: 266 us
  waiting for transfers between devices  156 us (58%)
  Pallas kernels  79.5 us (30%)
  starting transfers between devices  26.7 us (10%)
    pallas_call x17, Pallas kernels, call(): pl.pallas_call(body, out_shape=outs, in_specs=in_specs, out_specs=[places...  79.5 us
    ppermute x4, waiting for transfers between devices, trade(): lax.ppermute(part, 'replica', [(r, r ^ bit) for r in range(REPLICAS)])  73.6 us
    ppermute x8, waiting for transfers between devices, flow(): return lax.ppermute(shard, ('section', axis), pairs)  40.1 us
    ppermute x3, waiting for transfers between devices, to_other(): return lax.ppermute(shard, 'section', pairs)  35.5 us
    ppermute x8, starting transfers between devices, flow(): return lax.ppermute(shard, ('section', axis), pairs)  11.6 us
    ppermute x4, starting transfers between devices, trade(): lax.ppermute(part, 'replica', [(r, r ^ bit) for r in range(REPLICAS)])  8.17 us
    ppermute x2, waiting for transfers between devices, flow(): return lax.ppermute(shard, axis, pairs)  6.33 us
  transfers between devices with their start and end apart: 17, of which 12 were waited for; matrix products, arithmetic and copies ran while one was open for 0% of the time, Pallas kernels for 9%

profile of v2, /device:TPU:0, one launch (start us, length us, event | category | flops | bytes accessed | tf_op | source)
XLA Modules:
  0.0 266.0 jit_solution(3012807770621905802)
XLA Ops:
  1.5 11.7 %layer_forward.3 = (bf16[512,640]{1,0:T(8,128)(2,1)}, bf16[256,640]{1,0:T(8,128)(2,1)S(1)}, bf16[256,1920]{1,0:T(8,128)(2,1)S(1)}, bf16[20,256,256]{2,1,0:T(8,12...) custom-call(s32[4]{0:T(128)S(1)} %pad_add_fusion.info.refs_0_, ...), custom_call_target="tpu_custom_call" | custom-call | flops 115000000 | tf_op jit(solution)/shard_map/layer_forward/pallas_call | solution.py:128
  16.8 9.4 %layer_forward.4 = (bf16[512,640]{1,0:T(8,128)(2,1)}, bf16[256,640]{1,0:T(8,128)(2,1)S(1)}, bf16[256,1920]{1,0:T(8,128)(2,1)S(1)}, bf16[20,256,256]{2,1,0:T(8,12...) custom-call(s32[4]{0:T(128)S(1)} %pad_add_fusion.info.refs_0_, ...), custom_call_target="tpu_custom_call", output_to_operand_aliasing={{0}: (15, {})} | custom-call | flops 115000000 | tf_op jit(solution)/shard_map/layer_forward/pallas_call | solution.py:128
  26.3 2.3 collective-permute-start.1
  29.8 12.0 %layer_forward.5 = (bf16[512,640]{1,0:T(8,128)(2,1)}, bf16[256,640]{1,0:T(8,128)(2,1)}, bf16[256,1920]{1,0:T(8,128)(2,1)S(1)}, bf16[20,256,256]{2,1,0:T(8,128)(2...) custom-call(s32[4]{0:T(128)S(1)} %pad_add_fusion.info.refs_0_, ...), custom_call_target="tpu_custom_call", output_to_operand_aliasing={{0}: (14, {})} | custom-call | flops 115000000 | tf_op jit(solution)/shard_map/layer_forward/pallas_call | solution.py:128
  44.0 4.7 %attention_grad.2 = (bf16[512,640]{1,0:T(8,128)(2,1)}, bf16[512,1920]{1,0:T(8,128)(2,1)S(1)}, bf16[640,512]{1,0:T(8,128)(2,1)S(1)}, f32[16,640]{1,0:T(8,128)S(1)}, f32[8,128]{1,0:T(8,128)S(1)}) custom-call(s32[4]{0:T(128)S(1)} %pad_add_fusion.info.refs_0_, f32[512,640]{1,0:T(8,128)S(1)} %get-tuple-element.108.refs_1_, bf16[640,640]{1,0:T(8,128)(2,1)S(1)} %bitcast.36, ...), custom_call_target="tpu_custom_call" | custom-call | flops 13799999488 | tf_op jit(solution)/shard_map/attention_grad/pallas_call | solution.py:128
  53.5 33.0 %collective-permute-done.2.refs_3_ = bf16[512,640]{1,0:T(8,128)(2,1)S(1)} collective-permute-done((bf16[512,640]{1,0:T(8,128)(2,1)}, bf16[512,640]{1,0:T(8,128)(2,1)S(1)}, u32[]{:S(2)}, u32[]{:S(2)}) %collective-permute-start.2) | collective-permute-done | bytes 655392 | tf_op jit(solution)/shard_map/ppermute | solution.py:923
  86.6 13.1 %mlp_grad.3 = (bf16[1280,640]{1,0:T(8,128)(2,1)S(1)}, bf16[1280,640]{1,0:T(8,128)(2,1)S(1)}, bf16[1600,640]{1,0:T(8,128)(2,1)S(1)}, bf16[1600,640]{1,0:T(8,128)(...) custom-call(s32[4]{0:T(128)S(1)} %pad_add_fusion.info.refs_0_, ...), custom_call_target="tpu_custom_call" | custom-call | flops 11500000256 | tf_op jit(solution)/shard_map/mlp_grad/pallas_call | solution.py:128
  99.7 2.4 collective-permute-start.6
  102.1 2.2 collective-permute-start.5
  105.2 12.6 %attention_grad.3 = (bf16[512,640]{1,0:T(8,128)(2,1)}, bf16[512,1920]{1,0:T(8,128)(2,1)S(1)}, bf16[640,512]{1,0:T(8,128)(2,1)S(1)}, f32[16,640]{1,0:T(8,128)S(1)}, f32[8,128]{1,0:T(8,128)S(1)}) custom-call(s32[4]{0:T(128)S(1)} %pad_add_fusion.info.refs_0_, f32[512,640]{1,0:T(8,128)S(1)} %get-tuple-element.132.refs_1_, ...), custom_call_target="tpu_custom_call", output_to_operand_aliasing={{0}: (15, {})} | custom-call | flops 13799999488 | tf_op jit(solution)/shard_map/attention_grad/pallas_call | solution.py:128
  117.8 2.9 %qkv_grad.3 = (bf16[496,640]{1,0:T(8,128)(2,1)S(1)}, bf16[496,640]{1,0:T(8,128)(2,1)S(1)}, bf16[480,640]{1,0:T(8,128)(2,1)S(1)}, bf16[480,640]{1,0:T(8,128)(2,1)S(1)}, f32[8,128]{1,0:T(8,128)S(1)}) custom-call(s32[4]{0:T(128)S(1)} %pad_add_fusion.info.refs_0_, ...), custom_call_target="tpu_custom_call", output_to_operand_aliasing={{0}: (4, {}), {1}: (5, {}), {2}: (6, {}), {3}: (7, {})} | custom-call | flops 115000000 | tf_op jit(solution)/shard_map/qkv_grad/pallas_call | solution.py:128
  120.7 17.2 %collective-permute-done.5.refs_2_ = bf16[1280,640]{1,0:T(8,128)(2,1)S(1)} collective-permute-done((bf16[1280,640]{1,0:T(8,128)(2,1)S(1)}, bf16[1280,640]{1,0:T(8,128)(2,1)S(1)}, u32[]{:S(2)}, u32[]{:S(2)}) %collective-permute-start.5) | collective-permute-done | bytes 1638432 | tf_op jit(solution)/shard_map/ppermute | solution.py:874
  137.8 3.4 %collective-permute-done.6.refs_4_ = bf16[1600,640]{1,0:T(8,128)(2,1)S(1)} collective-permute-done((bf16[1600,640]{1,0:T(8,128)(2,1)S(1)}, bf16[1600,640]{1,0:T(8,128)(2,1)S(1)}, u32[]{:S(2)}, u32[]{:S(2)}) %collective-permute-start.6) | collective-permute-done | bytes 2048032 | tf_op jit(solution)/shard_map/ppermute | solution.py:874
  143.1 1.9 collective-permute-start.8
  145.8 1.9 collective-permute-start.7
  147.7 18.9 %collective-permute-done.7.refs_3_ = bf16[1120,640]{1,0:T(8,128)(2,1)S(1)} collective-permute-done((bf16[1120,640]{1,0:T(8,128)(2,1)S(1)}, bf16[1120,640]{1,0:T(8,128)(2,1)S(1)}, u32[]{:S(2)}, u32[]{:S(2)}) %collective-permute-start.7) | collective-permute-done | bytes 1433632 | tf_op jit(solution)/shard_map/ppermute | solution.py:874
  170.3 6.3 %collective-permute-done.12.refs_12_ = bf16[240,640]{1,0:T(8,128)(2,1)S(1)} collective-permute-done((bf16[240,640]{1,0:T(8,128)(2,1)S(1)}, bf16[240,640]{1,0:T(8,128)(2,1)S(1)}, u32[]{:S(2)}, u32[]{:S(2)}) %collective-permute-start.12) | collective-permute-done | bytes 307232 | tf_op jit(solution)/shard_map/ppermute | solution.py:871
  179.6 27.4 %collective-permute-done.13.two = bf16[992,640]{1,0:T(8,128)(2,1)S(1)} collective-permute-done((bf16[992,640]{1,0:T(8,128)(2,1)S(1)}, bf16[992,640]{1,0:T(8,128)(2,1)S(1)}, u32[]{:S(2)}, u32[]{:S(2)}) %collective-permute-start.13) | collective-permute-done | bytes 1269792 | tf_op jit(solution)/shard_map/ppermute | solution.py:729
  207.9 2.2 collective-permute-start.14
  210.0 14.9 %collective-permute-done.14.two = bf16[496,640]{1,0:T(8,128)(2,1)S(1)} collective-permute-done((bf16[496,640]{1,0:T(8,128)(2,1)S(1)}, bf16[496,640]{1,0:T(8,128)(2,1)S(1)}, u32[]{:S(2)}, u32[]{:S(2)}) %collective-permute-start.14) | collective-permute-done | bytes 634912 | tf_op jit(solution)/shard_map/ppermute | solution.py:729
  225.1 3.3 %collective-permute-start.15 = (bf16[496,640]{1,0:T(8,128)(2,1)S(1)}, bf16[496,640]{1,0:T(8,128)(2,1)S(1)}, u32[]{:S(2)}, u32[]{:S(2)}) collective-permute-start(bf16[496,640]{1,0:T(8,128)(2,1)S(1)} %total.1.one), channel_id=1, source_target_pairs={{0,2},{1,3},{2,0},{3,1},{4,6},{5,7},{6,4},{7,5},{8,10},{9,11},{10,... | collective-permute-start | bytes 1904648 | tf_op jit(solution)/shard_map/ppermute | solution.py:729
  228.4 15.1 %collective-permute-done.15.two = bf16[496,640]{1,0:T(8,128)(2,1)S(1)} collective-permute-done((bf16[496,640]{1,0:T(8,128)(2,1)S(1)}, bf16[496,640]{1,0:T(8,128)(2,1)S(1)}, u32[]{:S(2)}, u32[]{:S(2)}) %collective-permute-start.15) | collective-permute-done | bytes 634912 | tf_op jit(solution)/shard_map/ppermute | solution.py:729
  245.4 16.2 %collective-permute-done.16.refs_1_ = bf16[992,640]{1,0:T(8,128)(2,1)S(1)} collective-permute-done((bf16[992,640]{1,0:T(8,128)(2,1)S(1)}, bf16[992,640]{1,0:T(8,128)(2,1)S(1)}, u32[]{:S(2)}, u32[]{:S(2)}) %collective-permute-start.16) | collective-permute-done | bytes 1269792 | tf_op jit(solution)/shard_map/ppermute | solution.py:729
  261.5 4.3 %finish.1 = (f32[640,640]{1,0:T(8,128)}, f32[160,2560]{1,0:T(8,128)}, f32[160,640]{1,0:T(8,128)}, f32[160,1920]{1,0:T(8,128)}, f32[1,480]{1,0:T(1,128)}, /*index...) custom-call(s32[4]{0:T(128)S(1)} %pad_add_fusion.info.refs_0_, ...), custom_call_target="tpu_custom_call" | custom-call | flops 115000000 | tf_op jit(solution)/shard_map/finish/pallas_call | solution.py:128
  (90 shorter events, 24.6 us)
Async XLA Ops:
  14.2 2.5 collective-permute-start
  26.3 3.5 %collective-permute-start.1 = (bf16[256,640]{1,0:T(8,128)(2,1)S(1)}, bf16[256,640]{1,0:T(8,128)(2,1)S(1)}, u32[]{:S(2)}, u32[]{:S(2)}) collective-permute-start(bf16[256,640]{1,0:T(8,128)(2,1)S(1)} %get-tuple-element.97), channel_id=1, source_target_pairs={{0,16},{1,17},{2,18},{3,19},{4,20},{5,21},{6,22},{7,23},{8,24},{9,... | collective-permute-start | bytes 983048 | tf_op jit(solution)/shard_map/ppermute | solution.py:923
  42.4 8.1 %collective-permute-start.4 = (bf16[1600,640]{1,0:T(8,128)(2,1)S(1)}, bf16[1600,640]{1,0:T(8,128)(2,1)S(1)}, u32[]{:S(2)}, u32[]{:S(2)}) collective-permute-start(bf16[1600,640]{1,0:T(8,128)(2,1)S(1)} %get-tuple-element.123), channel_id=1, source_target_pairs={{16,24},{20,28},{24,16},{28,20},{17,25},{21,29},{25,17},{29,21},{1... | collective-permute-start | bytes 6144008 | tf_op jit(solution)/shard_map/ppermute | solution.py:874
  43.2 7.3 %collective-permute-start.3 = (bf16[1280,640]{1,0:T(8,128)(2,1)S(1)}, bf16[1280,640]{1,0:T(8,128)(2,1)S(1)}, u32[]{:S(2)}, u32[]{:S(2)}) collective-permute-start(bf16[1280,640]{1,0:T(8,128)(2,1)S(1)} %get-tuple-element.121), channel_id=1, source_target_pairs={{16,20},{20,16},{24,28},{28,24},{17,21},{21,17},{25,29},{29,25},{1... | collective-permute-start | bytes 4915208 | tf_op jit(solution)/shard_map/ppermute | solution.py:874
  48.7 37.8 %collective-permute-start.2 = (bf16[512,640]{1,0:T(8,128)(2,1)}, bf16[512,640]{1,0:T(8,128)(2,1)S(1)}, u32[]{:S(2)}, u32[]{:S(2)}) collective-permute-start(bf16[512,640]{1,0:T(8,128)(2,1)} %get-tuple-element.115.refs_15_), channel_id=1, source_target_pairs={{16,0},{17,1},{18,2},{19,3},{20,4},{21,5},{22,6},{23,7},{24,8},{25... | collective-permute-start | bytes 1966088 | tf_op jit(solution)/shard_map/ppermute | solution.py:923
  50.6 36.0 %copy-start.15 = (bf16[256,2560]{1,0:T(8,128)(2,1)S(1)}, bf16[256,2560]{1,0:T(8,128)(2,1)}, u32[]{:S(2)}) copy-start(bf16[256,2560]{1,0:T(8,128)(2,1)} %copy-done.14) | copy-start | bytes 3932164
  50.6 35.9 %copy-start.17 = (bf16[256,2560]{1,0:T(8,128)(2,1)S(1)}, bf16[256,2560]{1,0:T(8,128)(2,1)}, u32[]{:S(2)}) copy-start(bf16[256,2560]{1,0:T(8,128)(2,1)} %copy-done.16) | copy-start | bytes 3932164
  50.6 35.9 %copy-start.19 = (bf16[256,2560]{1,0:T(8,128)(2,1)S(1)}, bf16[256,2560]{1,0:T(8,128)(2,1)}, u32[]{:S(2)}) copy-start(bf16[256,2560]{1,0:T(8,128)(2,1)} %copy-done.18) | copy-start | bytes 3932164
  50.6 35.9 %copy-start.21 = (bf16[256,2560]{1,0:T(8,128)(2,1)S(1)}, bf16[256,2560]{1,0:T(8,128)(2,1)}, u32[]{:S(2)}) copy-start(bf16[256,2560]{1,0:T(8,128)(2,1)} %copy-done.20) | copy-start | bytes 3932164
  50.6 35.9 %copy-start.28 = (bf16[640,256]{1,0:T(8,128)(2,1)S(1)}, bf16[640,256]{1,0:T(8,128)(2,1)}, u32[]{:S(2)}) copy-start(bf16[640,256]{1,0:T(8,128)(2,1)} %copy-done.27) | copy-start | bytes 983044
  86.5 18.6 %copy-start.23 = (bf16[256,1920]{1,0:T(8,128)(2,1)S(1)}, bf16[256,1920]{1,0:T(8,128)(2,1)}, u32[]{:S(2)}) copy-start(bf16[256,1920]{1,0:T(8,128)(2,1)} %copy-done.22) | copy-start | bytes 2949124
  86.6 18.6 %copy-start.25 = (bf16[256,1920]{1,0:T(8,128)(2,1)S(1)}, bf16[256,1920]{1,0:T(8,128)(2,1)}, u32[]{:S(2)}) copy-start(bf16[256,1920]{1,0:T(8,128)(2,1)} %copy-done.24) | copy-start | bytes 2949124
  99.7 41.6 %collective-permute-start.6 = (bf16[1600,640]{1,0:T(8,128)(2,1)S(1)}, bf16[1600,640]{1,0:T(8,128)(2,1)S(1)}, u32[]{:S(2)}, u32[]{:S(2)}) collective-permute-start(bf16[1600,640]{1,0:T(8,128)(2,1)S(1)} %get-tuple-element.141), channel_id=1, source_target_pairs={{0,8},{4,12},{8,0},{12,4},{1,9},{5,13},{9,1},{13,5},{2,10},{6,14},... | collective-permute-start | bytes 6144008 | tf_op jit(solution)/shard_map/ppermute | solution.py:874
  102.1 35.7 %collective-permute-start.5 = (bf16[1280,640]{1,0:T(8,128)(2,1)S(1)}, bf16[1280,640]{1,0:T(8,128)(2,1)S(1)}, u32[]{:S(2)}, u32[]{:S(2)}) collective-permute-start(bf16[1280,640]{1,0:T(8,128)(2,1)S(1)} %get-tuple-element.139), channel_id=1, source_target_pairs={{0,4},{4,0},{8,12},{12,8},{1,5},{5,1},{9,13},{13,9},{2,6},{6,2},{1... | collective-permute-start | bytes 4915208 | tf_op jit(solution)/shard_map/ppermute | solution.py:874
  104.4 43.3 %collective-permute-start.10 = (bf16[1296,640]{1,0:T(8,128)(2,1)}, bf16[1296,640]{1,0:T(8,128)(2,1)S(1)}, u32[]{:S(2)}, u32[]{:S(2)}) collective-permute-start(bf16[1296,640]{1,0:T(8,128)(2,1)} %get-tuple-element.157), channel_id=1, source_target_pairs={{16,20},{20,16},{24,28},{28,24},{17,21},{21,17},{25,29},{29,25},{1... | collective-permute-start | bytes 4976648 | tf_op jit(solution)/shard_map/ppermute | solution.py:874
  143.1 24.1 %collective-permute-start.8 = (bf16[1296,640]{1,0:T(8,128)(2,1)S(1)}, bf16[1296,640]{1,0:T(8,128)(2,1)S(1)}, u32[]{:S(2)}, u32[]{:S(2)}) collective-permute-start(bf16[1296,640]{1,0:T(8,128)(2,1)S(1)} %get-tuple-element.154), channel_id=1, source_target_pairs={{0,4},{4,0},{8,12},{12,8},{1,5},{5,1},{9,13},{13,9},{2,6},{6,2},{1... | collective-permute-start | bytes 4976648 | tf_op jit(solution)/shard_map/ppermute | solution.py:874
  145.0 2.7 %collective-permute-start.9 = (bf16[1120,640]{1,0:T(8,128)(2,1)S(1)}, bf16[1120,640]{1,0:T(8,128)(2,1)S(1)}, u32[]{:S(2)}, u32[]{:S(2)}) collective-permute-start(bf16[1120,640]{1,0:T(8,128)(2,1)S(1)} %copy-done.13), channel_id=1, source_target_pairs={{16,24},{20,28},{24,16},{28,20},{17,25},{21,29},{25,17},{29,21},{1... | collective-permute-start | bytes 4300808 | tf_op jit(solution)/shard_map/ppermute | solution.py:874
  145.8 20.8 %collective-permute-start.7 = (bf16[1120,640]{1,0:T(8,128)(2,1)S(1)}, bf16[1120,640]{1,0:T(8,128)(2,1)S(1)}, u32[]{:S(2)}, u32[]{:S(2)}) collective-permute-start(bf16[1120,640]{1,0:T(8,128)(2,1)S(1)} %get-tuple-element.153), channel_id=1, source_target_pairs={{0,8},{4,12},{8,0},{12,4},{1,9},{5,13},{9,1},{13,5},{2,10},{6,14},... | collective-permute-start | bytes 4300808 | tf_op jit(solution)/shard_map/ppermute | solution.py:874
  168.2 8.4 %collective-permute-start.11 = (bf16[256,640]{1,0:T(8,128)(2,1)S(1)}, bf16[256,640]{1,0:T(8,128)(2,1)S(1)}, u32[]{:S(2)}, u32[]{:S(2)}) collective-permute-start(bf16[256,640]{1,0:T(8,128)(2,1)S(1)} %get-tuple-element.162), channel_id=1, source_target_pairs={{0,8},{4,12},{8,0},{12,4},{1,9},{5,13},{9,1},{13,5},{2,10},{6,14},... | collective-permute-start | bytes 983048 | tf_op jit(solution)/shard_map/ppermute | solution.py:871
  169.8 6.9 %collective-permute-start.12 = (bf16[240,640]{1,0:T(8,128)(2,1)S(1)}, bf16[240,640]{1,0:T(8,128)(2,1)S(1)}, u32[]{:S(2)}, u32[]{:S(2)}) collective-permute-start(bf16[240,640]{1,0:T(8,128)(2,1)S(1)} %get-tuple-element.163), channel_id=1, source_target_pairs={{0,4},{4,0},{8,12},{12,8},{1,5},{5,1},{9,13},{13,9},{2,6},{6,2},{1... | collective-permute-start | bytes 921608 | tf_op jit(solution)/shard_map/ppermute | solution.py:871
  177.9 29.0 %collective-permute-start.13 = (bf16[992,640]{1,0:T(8,128)(2,1)S(1)}, bf16[992,640]{1,0:T(8,128)(2,1)S(1)}, u32[]{:S(2)}, u32[]{:S(2)}) collective-permute-start(bf16[992,640]{1,0:T(8,128)(2,1)S(1)} %get-tuple-element.165), channel_id=1, source_target_pairs={{0,1},{1,0},{2,3},{3,2},{4,5},{5,4},{6,7},{7,6},{8,9},{9,8},{10,11... | collective-permute-start | bytes 3809288 | tf_op jit(solution)/shard_map/ppermute | solution.py:729
  207.9 17.1 %collective-permute-start.14 = (bf16[496,640]{1,0:T(8,128)(2,1)S(1)}, bf16[496,640]{1,0:T(8,128)(2,1)S(1)}, u32[]{:S(2)}, u32[]{:S(2)}) collective-permute-start(bf16[496,640]{1,0:T(8,128)(2,1)S(1)} %get-tuple-element.167), channel_id=1, source_target_pairs={{0,2},{1,3},{2,0},{3,1},{4,6},{5,7},{6,4},{7,5},{8,10},{9,11},{10,... | collective-permute-start | bytes 1904648 | tf_op jit(solution)/shard_map/ppermute | solution.py:729
  225.1 18.4 %collective-permute-start.15 = (bf16[496,640]{1,0:T(8,128)(2,1)S(1)}, bf16[496,640]{1,0:T(8,128)(2,1)S(1)}, u32[]{:S(2)}, u32[]{:S(2)}) collective-permute-start(bf16[496,640]{1,0:T(8,128)(2,1)S(1)} %total.1.one), channel_id=1, source_target_pairs={{0,2},{1,3},{2,0},{3,1},{4,6},{5,7},{6,4},{7,5},{8,10},{9,11},{10,... | collective-permute-start | bytes 1904648 | tf_op jit(solution)/shard_map/ppermute | solution.py:729
  244.3 17.2 %collective-permute-start.16 = (bf16[992,640]{1,0:T(8,128)(2,1)S(1)}, bf16[992,640]{1,0:T(8,128)(2,1)S(1)}, u32[]{:S(2)}, u32[]{:S(2)}) collective-permute-start(bf16[992,640]{1,0:T(8,128)(2,1)S(1)} %double.1.refs_0_), channel_id=1, source_target_pairs={{0,1},{1,0},{2,3},{3,2},{4,5},{5,4},{6,7},{7,6},{8,9},{9,8},{10,11... | collective-permute-start | bytes 3809288 | tf_op jit(solution)/shard_map/ppermute | solution.py:729
  (24 other events, 300.7 us)
